TPU v7x, 256 devices: a whole 4x4x8 slice. The times are simulated.
256 devices in a mesh: seq: 32 (over y_hi, z, core), ch: 8 (over y_lo, x).
Axes of the slice: x: 4, y: 4 (y_hi: 2, y_lo: 2; y = y_hi * 2 + y_lo), z: 8, core: 2. Of those that a mesh axis runs over, the one named last changes fastest.
Arguments:
- cotangent: bfloat16 [4096, 4096], P('seq', 'ch'), may hold values from -6 to 6
- keep_mask: int32 [4096, 4096], P('seq', 'ch'), may hold values 0 or 1
- gate_out: bfloat16 [4096, 4096], P('seq', 'ch'), may hold values from -6 to 6
- gate_in: bfloat16 [4096, 4096], P('seq', 'ch'), may hold values from -6 to 6
- value_in: bfloat16 [4096, 4096], P('seq', 'ch'), may hold values from -6 to 6
- filter_taps: float32 [4096, 4096], P('seq', 'ch'), may hold values from -3 to 3
- out_weight: bfloat16 [4096, 4096], P('seq', 'ch'), may hold values from -0.09375 to 0.09375
Outputs:
- grad_gate_out: bfloat16 [4096, 4096], P('seq', 'ch')
- grad_gate_in: bfloat16 [4096, 4096], P('seq', 'ch')
- grad_value: bfloat16 [4096, 4096], P('seq', 'ch')
- grad_filter: float32 [4096, 4096], P('seq', 'ch')
- grad_weight: float32 [4096, 4096], P('seq', 'ch')
All inputs are finite; a program needn't handle non-finite values. No bound on the sum of `keep_mask` on one device may be relied on, other than what follows from the above.
Results may differ from a plain program's by a relative error of at most 0.023.
Values may be sent and summed in bfloat16 or wider, within the bound.
No kernel may reach another device: no remote copies, remote signals or barrier semaphores. Data moves between devices by JAX's collectives and lax.ppermute only.
A program may use at most 64 MiB of HBM per device.

v0:
```python
import math

import jax
import jax.numpy as jnp
from jax import lax
from jax.sharding import PartitionSpec as P

keep_prob = 0.9


def as_sent(array):
    return jax.tree.map(lambda a: a.astype(jnp.bfloat16) if a.dtype == jnp.float32 else a, array)


def rotation_table(size_now, direction):
    indices = jnp.arange(size_now, dtype=jnp.int32)
    phases = (indices[:, None] * indices[None, :] % size_now).astype(jnp.float32)
    angles = direction * 2.0 * math.pi / size_now * phases
    cosine = jnp.cos(angles)
    sine_table = jnp.sin(angles)
    return jnp.stack([jnp.stack([cosine, sine_table]), jnp.stack([-sine_table, cosine])])


def transform(stacked, direction, upper_zero=False):
    length = stacked.shape[-1]
    highest = lax.Precision.HIGHEST
    if length <= 256:
        table = rotation_table(length, direction)
        return jnp.einsum("c...b,cdbk->d...k", stacked, table, precision=highest)
    factor = 32
    inner_len = length // factor
    leading = stacked.shape[1:-1]
    shaped = stacked.reshape((2,) + leading + (factor, inner_len))
    table = rotation_table(factor, direction)
    if upper_zero:
        shaped = shaped[..., : factor // 2, :]
        table = table[:, :, : factor // 2]
    section = jnp.einsum("c...ab,cdak->d...kb", shaped, table, precision=highest)
    first_index = jnp.arange(factor, dtype=jnp.int32)
    second_index = jnp.arange(inner_len, dtype=jnp.int32)
    phases = (first_index[:, None] * second_index[None, :] % length).astype(jnp.float32)
    angles = direction * 2.0 * math.pi / length * phases
    twist_cos = jnp.cos(angles)
    twist_sin = jnp.sin(angles)
    turned_real = section[0] * twist_cos - section[1] * twist_sin
    turned_imag = section[0] * twist_sin + section[1] * twist_cos
    sub_parts = transform(jnp.stack([turned_real, turned_imag]), direction)
    return jnp.swapaxes(sub_parts, -1, -2).reshape((2,) + leading + (length,))


def padded_rows(local_rows):
    return jnp.concatenate([local_rows, jnp.zeros_like(local_rows)], axis=1)


def spectrum(local_rows):
    padded = padded_rows(local_rows)
    result = transform(jnp.stack([padded, jnp.zeros_like(padded)]), -1.0, True)
    return (result[0], result[1])


def reversed_index(values):
    return jnp.roll(jnp.flip(values, axis=-1), 1, axis=-1)


def spectrum_pair(first_rows, second_rows):
    joint = transform(jnp.stack([padded_rows(first_rows), padded_rows(second_rows)]), -1.0, True)
    joint_real = joint[0]
    joint_imag = joint[1]
    mirror_real = reversed_index(joint_real)
    mirror_imag = reversed_index(joint_imag)
    first_spec = (0.5 * (joint_real + mirror_real), 0.5 * (joint_imag - mirror_imag))
    second_spec = (0.5 * (joint_imag + mirror_imag), 0.5 * (mirror_real - joint_real))
    return (first_spec, second_spec)


def times_conj(left, right, conjugate):
    if conjugate:
        return (left[0] * right[0] + left[1] * right[1], left[1] * right[0] - left[0] * right[1])
    return (left[0] * right[0] - left[1] * right[1], left[0] * right[1] + left[1] * right[0])


def inverse(freq, keep_len):
    result = transform(jnp.stack([freq[0], freq[1]]), 1.0)
    return result[0][:, :keep_len] / freq[0].shape[-1]


def inverse_pair(first_freq, second_freq, keep_len):
    total = first_freq[0].shape[-1]
    result = transform(
        jnp.stack([first_freq[0] - second_freq[1], first_freq[1] + second_freq[0]]), 1.0
    )
    return (result[0][:, :keep_len] / total, result[1][:, :keep_len] / total)


def body(cotangent, keep_mask, gate_out, gate_in, value_in, filter_taps, out_weight):
    shards = lax.axis_size("seq")
    tok_rows = cotangent.shape[0]
    tokens_all = tok_rows * shards
    scale_back = 1.0 / math.sqrt(tokens_all)
    product = (gate_in.astype(jnp.float32) * value_in.astype(jnp.float32)).astype(jnp.bfloat16)
    dropped = (cotangent.astype(jnp.float32) * keep_mask.astype(jnp.float32) / keep_prob).astype(
        jnp.bfloat16
    )
    cot_full = lax.all_gather(dropped, "ch", axis=1, tiled=True)
    taps_local = lax.all_to_all(
        filter_taps.T.astype(jnp.bfloat16), "seq", split_axis=0, concat_axis=1, tiled=True
    ).astype(jnp.float32)
    columns = cot_full
    grad_mixed = jnp.dot(
        columns,
        lax.all_gather(out_weight, "seq", axis=0, tiled=True),
        preferred_element_type=jnp.float32,
    )
    conv_grad = (grad_mixed * gate_out.astype(jnp.float32)).astype(jnp.bfloat16)
    prod_local, grad_local = (
        lax.all_to_all(product.T, "seq", split_axis=0, concat_axis=1, tiled=True),
        lax.all_to_all(conv_grad.T, "seq", split_axis=0, concat_axis=1, tiled=True),
    )
    taps_spec, prod_spec = spectrum_pair(taps_local, prod_local.astype(jnp.float32))
    grad_spec = spectrum(grad_local.astype(jnp.float32))
    conv_local = inverse(times_conj(taps_spec, prod_spec, False), tokens_all).astype(jnp.bfloat16)
    back_full, filter_full = inverse_pair(
        times_conj(grad_spec, taps_spec, True), times_conj(grad_spec, prod_spec, True), tokens_all
    )
    back_local = back_full.astype(jnp.bfloat16)
    conv_rows, back_rows = (
        lax.all_to_all(conv_local, "seq", split_axis=1, concat_axis=0, tiled=True),
        lax.all_to_all(back_local, "seq", split_axis=1, concat_axis=0, tiled=True),
    )
    filter_local = filter_full * scale_back
    filter_rows = lax.all_to_all(
        as_sent(filter_local), "seq", split_axis=1, concat_axis=0, tiled=True
    ).astype(filter_local.dtype)
    grad_filter = filter_rows.T
    conv = conv_rows.T
    back = back_rows.T
    mixed_act = (gate_out.astype(jnp.float32) * conv.astype(jnp.float32)).astype(jnp.bfloat16)
    columns = cot_full
    grad_weight = (
        lax.psum_scatter(
            lax.dot_general(
                columns, mixed_act, (((0,), (0,)), ((), ())), preferred_element_type=jnp.float32
            ).astype(jnp.bfloat16),
            "seq",
            scatter_dimension=0,
            tiled=True,
        ).astype(jnp.float32)
        * scale_back
    )
    grad_gate_out = (grad_mixed * conv.astype(jnp.float32)).astype(jnp.bfloat16)
    grad_gate_in = (back.astype(jnp.float32) * value_in.astype(jnp.float32)).astype(jnp.bfloat16)
    grad_value = (back.astype(jnp.float32) * gate_in.astype(jnp.float32)).astype(jnp.bfloat16)
    return (grad_gate_out, grad_gate_in, grad_value, grad_filter, grad_weight)


def solution(mesh):
    in_specs = (
        P("seq", "ch"),
        P("seq", "ch"),
        P("seq", "ch"),
        P("seq", "ch"),
        P("seq", "ch"),
        P("seq", "ch"),
        P("seq", "ch"),
    )
    out_specs = (P("seq", "ch"), P("seq", "ch"), P("seq", "ch"), P("seq", "ch"), P("seq", "ch"))
    return jax.shard_map(body, mesh=mesh, in_specs=in_specs, out_specs=out_specs, check_vma=False)
```

profile of v0, /device:TPU:2, one launch (start us, length us, event | category | flops | bytes accessed | tf_op | source)
XLA Modules:
  0.0 388.0 jit_solution(18346484520013370987)
XLA Ops:
  12.5 11.5 %all-to-all-start.1 = ((bf16[32,16,128]{2,1,0:T(8,128)(2,1)}), bf16[32,16,128]{2,1,0:T(8,128)(2,1)S(1)}, u32[]{:S(2)}, u32[]{:S(2)}) async-start(bf16[32,16,128]{2,1,0:T(8,128)(2,1)} %bitcast.20), calls=%async_computation.1 | async-start | bytes 262144 | tf_op jit(solution)/shard_map/all_to_all | solution.py:116
  33.1 2.8 all-to-all-done.1
  35.9 7.0 %all-to-all-start = ((bf16[32,16,128]{2,1,0:T(8,128)(2,1)}), bf16[32,16,128]{2,1,0:T(8,128)(2,1)S(1)}, u32[]{:S(2)}, u32[]{:S(2)}) async-start(bf16[32,16,128]{2,1,0:T(8,128)(2,1)} %bitcast.17), calls=%async_computation | async-start | bytes 262144 | tf_op jit(solution)/shard_map/all_to_all | solution.py:105
  43.0 9.7 %all-gather.3.cloned.1.call-done = bf16[128,4096]{1,0:T(8,128)(2,1)} async-done(((bf16[128,512]{1,0:T(8,128)(2,1)}), bf16[128,4096]{1,0:T(8,128)(2,1)}) %all-gather.3.cloned.1.call-update) | async-done | bytes 1048592 | tf_op jit(solution)/shard_map/all_gather | solution.py:104
  52.7 91.6 %all-gather.5.cloned.1.call-done = bf16[4096,512]{1,0:T(8,128)(2,1)} async-done(((bf16[128,512]{1,0:T(8,128)(2,1)}), bf16[4096,512]{1,0:T(8,128)(2,1)}) %all-gather.5.cloned.1.call-update) | async-done | bytes 4194320 | tf_op jit(solution)/shard_map/all_gather | solution.py:111
  144.2 3.2 fusion.79
  148.3 4.6 %all-to-all-start.3 = ((bf16[32,16,128]{2,1,0:T(8,128)(2,1)}), bf16[32,16,128]{2,1,0:T(8,128)(2,1)S(1)}, u32[]{:S(2)}, u32[]{:S(2)}) async-start(bf16[32,16,128]{2,1,0:T(8,128)(2,1)} %bitcast.57), calls=%async_computation.3 | async-start | bytes 262144 | tf_op jit(solution)/shard_map/all_to_all | solution.py:117
  154.7 10.2 %all-to-all-done.3 = bf16[32,16,128]{2,1,0:T(8,128)(2,1)S(1)} async-done(((bf16[32,16,128]{2,1,0:T(8,128)(2,1)}), bf16[32,16,128]{2,1,0:T(8,128)(2,1)S(1)}, u32[]{:S(2)}, u32[]{:S(2)}) %all-to-all-start.3) | async-done | bytes 131104 | tf_op jit(solution)/shard_map/all_to_all | solution.py:117
  166.4 2.1 multiply_subtract_fusion.4
  168.5 1.9 convolution_bitcast_fusion.6
  176.3 2.0 slice.140
  182.4 2.0 slice.143
  186.5 3.1 convolution_bitcast_fusion.2
  194.0 24.9 %reverse.5 = f32[16,8192]{1,0:T(8,128)S(1)} reverse(f32[16,8192]{1,0:T(8,128)} %bitcast.297), dimensions={1} | reverse | bytes 1048576
  220.3 4.6 %reverse.4 = f32[16,8192]{1,0:T(8,128)S(1)} reverse(f32[16,8192]{1,0:T(8,128)S(1)} %bitcast.296), dimensions={1} | reverse | bytes 1048576
  230.8 1.9 convolution_bitcast_fusion.4
  237.9 14.9 %all_to_all.78 = bf16[16,32,128]{2,0,1:T(8,128)(2,1)S(1)} all-to-all(bf16[16,32,128]{2,0,1:T(8,128)(2,1)S(1)} %copy_bitcast_fusion.7), channel_id=1, replica_groups=mesh['seq'=32,'ch'=8] {'seq'}, dimensions={1} | all-to-all | bytes 262144 | tf_op jit(solution)/shard_map/all_to_all | solution.py:127
  253.0 4.1 %convolution_convert_fusion = bf16[4096,512]{1,0:T(8,128)(2,1)} fusion(bf16[128,4096]{1,0:T(8,128)(2,1)S(1)} %copy-done, bf16[128,512]{1,0:T(8,128)(2,1)} %param.9, f32[512,128]{0,1:T(8,128)S(1)} %copy.145), kind=kOutput, calls=%fused_computation | convolution fusion | flops 539164672 | bytes 5636096 | tf_op jit(solution)/shard_map/dot_general | solution.py:141
  258.7 1.9 convolution_bitcast_fusion
  266.5 3.9 all-to-all-start.4
  272.6 9.7 %all-to-all-done.4 = bf16[16,32,128]{2,0,1:T(8,128)(2,1)S(1)} async-done(((bf16[16,32,128]{2,0,1:T(8,128)(2,1)}), bf16[16,32,128]{2,0,1:T(8,128)(2,1)S(1)}, u32[]{:S(2)}, u32[]{:S(2)}) %all-to-all-start.4) | async-done | bytes 131104 | tf_op jit(solution)/shard_map/all_to_all | solution.py:128
  282.3 3.9 all-to-all-start.5
  287.8 10.3 %all-to-all-done.5 = bf16[16,32,128]{2,0,1:T(8,128)(2,1)S(1)} async-done(((bf16[16,32,128]{2,0,1:T(8,128)(2,1)}), bf16[16,32,128]{2,0,1:T(8,128)(2,1)S(1)}, u32[]{:S(2)}, u32[]{:S(2)}) %all-to-all-start.5) | async-done | bytes 131104 | tf_op jit(solution)/shard_map/all_to_all | solution.py:131
  299.7 80.1 %reduce-scatter.2.cloned.1.call-done = bf16[128,512]{1,0:T(8,128)(2,1)} async-done(((bf16[4096,512]{1,0:T(8,128)(2,1)}), bf16[128,512]{1,0:T(8,128)(2,1)}) %reduce-scatter.2.cloned.1.call-update) | async-done | bytes 131088 | tf_op jit(solution)/shard_map/reduce_scatter | solution.py:140
  (121 shorter events, 61.8 us)
Async XLA Ops:
  7.2 23.5 %copy-start.15 = (f32[128,512]{1,0:T(8,128)S(1)}, f32[128,512]{1,0:T(8,128)}, u32[]{:S(2)}) copy-start(f32[128,512]{1,0:T(8,128)} %param.12) | copy-start | bytes 786436
  7.2 45.5 %all-gather.3.cloned.1.call-start = ((), (), s32[]{:S(2)}) async-start(), calls=%async_computation.7 | async-start | bytes 1179648 | tf_op jit(solution)/shard_map/all_gather | solution.py:104
  9.0 135.3 %all-gather.5.cloned.1.call-start = ((), (), s32[]{:S(2)}) async-start(), calls=%async_computation.8 | async-start | bytes 4325376 | tf_op jit(solution)/shard_map/all_gather | solution.py:111
  11.8 18.7 %copy-start.4 = (bf16[128,512]{0,1:T(8,128)(2,1)}, bf16[128,512]{0,1:T(8,128)(2,1)S(1)}, u32[]{:S(2)}) copy-start(bf16[128,512]{0,1:T(8,128)(2,1)S(1)} %copy.126) | copy-start | bytes 393220
  12.5 23.5 %all-to-all-start.1 = ((bf16[32,16,128]{2,1,0:T(8,128)(2,1)}), bf16[32,16,128]{2,1,0:T(8,128)(2,1)S(1)}, u32[]{:S(2)}, u32[]{:S(2)}) async-start(bf16[32,16,128]{2,1,0:T(8,128)(2,1)} %bitcast.20), calls=%async_computation.1 | async-start | bytes 262144 | tf_op jit(solution)/shard_map/all_to_all | solution.py:116
  30.7 116.8 %copy-start.6 = (bf16[128,512]{1,0:T(8,128)(2,1)S(1)}, bf16[128,512]{1,0:T(8,128)(2,1)}, u32[]{:S(2)}) copy-start(bf16[128,512]{1,0:T(8,128)(2,1)} %param.9) | copy-start | bytes 393220
  35.9 112.3 %all-to-all-start = ((bf16[32,16,128]{2,1,0:T(8,128)(2,1)}), bf16[32,16,128]{2,1,0:T(8,128)(2,1)S(1)}, u32[]{:S(2)}, u32[]{:S(2)}) async-start(bf16[32,16,128]{2,1,0:T(8,128)(2,1)} %bitcast.17), calls=%async_computation | async-start | bytes 262144 | tf_op jit(solution)/shard_map/all_to_all | solution.py:105
  148.3 16.6 %all-to-all-start.3 = ((bf16[32,16,128]{2,1,0:T(8,128)(2,1)}), bf16[32,16,128]{2,1,0:T(8,128)(2,1)S(1)}, u32[]{:S(2)}, u32[]{:S(2)}) async-start(bf16[32,16,128]{2,1,0:T(8,128)(2,1)} %bitcast.57), calls=%async_computation.3 | async-start | bytes 262144 | tf_op jit(solution)/shard_map/all_to_all | solution.py:117
  152.9 226.9 %reduce-scatter.2.cloned.1.call-start = ((), (), s32[]{:S(2)}) async-start(), calls=%async_computation.9 | async-start | bytes 4325376 | tf_op jit(solution)/shard_map/reduce_scatter | solution.py:140
  193.9 26.3 %copy-start.1 = (f32[16,8191]{1,0:T(8,128)S(1)}, f32[16,8191]{1,0:T(8,128)}, u32[]{:S(2)}) copy-start(f32[16,8191]{1,0:T(8,128)} %slice.143) | copy-start | bytes 1572676
  194.0 31.5 %copy-start.2 = (f32[1,16,32,256]{3,2,1,0:T(8,128)S(1)}, f32[1,16,32,256]{3,2,1,0:T(8,128)}, u32[]{:S(2)}) copy-start(f32[1,16,32,256]{3,2,1,0:T(8,128)} %squeeze.18) | copy-start | bytes 1572868
  220.2 5.2 %copy-start.3 = (f32[2,8,32,256]{3,2,1,0:T(8,128)S(1)}, f32[2,8,32,256]{3,2,1,0:T(8,128)}, u32[]{:S(2)}) copy-start(f32[2,8,32,256]{3,2,1,0:T(8,128)} %copy.202) | copy-start | bytes 1572868
  225.5 1.9 copy-start.13
  225.5 1.9 copy-start.14
  227.0 2.5 copy-start.16
  227.0 2.5 copy-start.17
  227.4 3.4 copy-start.7
  227.4 3.4 copy-start.9
  232.7 20.3 %copy-start = (bf16[128,4096]{1,0:T(8,128)(2,1)S(1)}, bf16[128,4096]{1,0:T(8,128)(2,1)}, u32[]{:S(2)}) copy-start(bf16[128,4096]{1,0:T(8,128)(2,1)} %all-gather.3.cloned.1.call-done) | copy-start | bytes 3145732
  257.2 1.4 copy-start.11
  257.2 1.5 copy-start.12
  263.1 23.1 %copy-start.5 = (bf16[128,512]{0,1:T(8,128)(2,1)S(1)}, bf16[128,512]{0,1:T(8,128)(2,1)}, u32[]{:S(2)}) copy-start(bf16[128,512]{0,1:T(8,128)(2,1)} %copy-done.4) | copy-start | bytes 393220
  266.5 15.8 %all-to-all-start.4 = ((bf16[16,32,128]{2,0,1:T(8,128)(2,1)}), bf16[16,32,128]{2,0,1:T(8,128)(2,1)S(1)}, u32[]{:S(2)}, u32[]{:S(2)}) async-start(bf16[16,32,128]{2,0,1:T(8,128)(2,1)} %copy_bitcast_fusion.6), calls=%async_computation.4 | async-start | bytes 262144 | tf_op jit(solution)/shard_map/all_to_all | solution.py:128
  282.3 15.8 %all-to-all-start.5 = ((bf16[16,32,128]{2,0,1:T(8,128)(2,1)}), bf16[16,32,128]{2,0,1:T(8,128)(2,1)S(1)}, u32[]{:S(2)}, u32[]{:S(2)}) async-start(bf16[16,32,128]{2,0,1:T(8,128)(2,1)} %copy_bitcast_fusion.5), calls=%async_computation.5 | async-start | bytes 262144 | tf_op jit(solution)/shard_map/all_to_all | solution.py:131
  (2 other events, 2.2 us)
Sparse Core Ops, SparseCore 0:
  10.4 42.2 all-gather.2
  55.4 88.7 all-gather.4
  257.3 122.4 reduce-scatter.1
where the time goes:
time: 391 us; the launch traced here: 388 us
  waiting for transfers between devices  215 us (55%)
  local copies, waits for them, and re-layouts  69.5 us (18%)
  starting transfers between devices  31.1 us (8%)
  other arithmetic  22.1 us (6%)
  matrix products  20.8 us (5%)
  blocking collectives  14.9 us (4%)
  between operations  14.3 us (4%)
    all_gather x1, waiting for transfers between devices, body(): lax.all_gather(out_weight, 'seq', axis=0, tiled=True)  91.6 us
    reduce_scatter x1, waiting for transfers between devices, body(): lax.psum_scatter(lax.dot_general(columns, mixed_act, (((0,), (0,)), ((),...  80.1 us
    unnamed x49, local copies, waits for them, and re-layouts  37.5 us
    all_to_all x1, blocking collectives, body(): lax.all_to_all(conv_local, 'seq', split_axis=1, concat_axis=0, tiled=True)  14.9 us
    all_to_all x1, starting transfers between devices, body(): lax.all_to_all(product.T, 'seq', split_axis=0, concat_axis=1, tiled=True)  11.5 us
    all_to_all x1, waiting for transfers between devices, body(): lax.all_to_all(as_sent(filter_local), 'seq', split_axis=1, concat_axis=0,...  10.3 us
    all_to_all x1, waiting for transfers between devices, body(): lax.all_to_all(conv_grad.T, 'seq', split_axis=0, concat_axis=1, tiled=True)  10.2 us
    all_to_all x1, waiting for transfers between devices, body(): lax.all_to_all(back_local, 'seq', split_axis=1, concat_axis=0, tiled=True)  9.7 us
  transfers between devices with their start and end apart: 8, of which 7 were waited for; matrix products, arithmetic and copies ran while one was open for 8% of the time, Pallas kernels for 0%

commit v1 on v0

v1 whole, which is shorter than its diff:
```python
import math
import jax, jax.numpy as jnp, numpy as np, ml_dtypes
from jax import lax
from jax.sharding import Mesh, PartitionSpec as P
from jax.experimental import pallas as pl
from jax.experimental.pallas import tpu as pltpu

BF = jnp.bfloat16
F32 = jnp.float32
BLK = 128
NBLK = 32
GRP = 16
FRQ = 40
LEN = 2 * BLK * NBLK


def split_np(table):
    hi = table.astype(ml_dtypes.bfloat16)
    lo = (table - hi.astype(np.float64)).astype(ml_dtypes.bfloat16)
    return hi, lo


def tables():
    f1 = np.arange(FRQ)[:, None]
    live = (f1 <= NBLK).astype(np.float64)
    k = np.arange(NBLK)[None, :]
    ang = 2 * np.pi * ((f1 * k) % (2 * NBLK)) / (2 * NBLK)
    first = np.concatenate([np.cos(ang) * live, -np.sin(ang) * live], 0)
    weight = np.where((f1 == 0) | (f1 == NBLK), 1.0, 2.0) * live / LEN
    last = np.concatenate([np.cos(ang) * weight, -np.sin(ang) * weight], 0).T
    s = np.arange(BLK)
    turn = 2 * np.pi * (f1 * s[None, :]) / LEN
    ang2 = 2 * np.pi * ((s[:, None] * s[None, :]) % BLK) / BLK
    c, d = np.cos(ang2), np.sin(ang2)
    fwd = np.block([[c, -d], [d, c]])
    inv = np.block([[c, d], [-d, c]])
    first = np.concatenate(split_np(first), 0)
    last = np.concatenate(split_np(last), 0)
    return (first, np.cos(turn).astype(np.float32), np.sin(turn).astype(np.float32),
            *split_np(fwd), *split_np(inv), last)


def split(x):
    hi = x.astype(BF)
    return hi, (x - hi.astype(F32)).astype(BF)


def dot(a, b):
    return jnp.dot(a, b, preferred_element_type=F32)


def wide_dot(x, hi_tab, lo_tab):
    hi, lo = split(x)
    return dot(hi, hi_tab) + dot(lo, hi_tab) + dot(hi, lo_tab)


def to_freq(src, rows, work, first, cos_t, sin_t, fwd_hi, fwd_lo):
    rows[...] = src.astype(F32).reshape(NBLK * GRP, BLK)
    lanes = jnp.concatenate([rows[pl.ds(g, NBLK, stride=GRP), :] for g in range(GRP)], axis=1).astype(BF)
    both = dot(first, lanes)
    part = both[: 2 * FRQ] + both[2 * FRQ:]
    for g in range(GRP):
        re = part[:FRQ, g * BLK:(g + 1) * BLK]
        im = part[FRQ:, g * BLK:(g + 1) * BLK]
        work[g * FRQ:(g + 1) * FRQ, :BLK] = re * cos_t + im * sin_t
        work[g * FRQ:(g + 1) * FRQ, BLK:] = im * cos_t - re * sin_t
    return wide_dot(work[...], fwd_hi, fwd_lo)


def from_freq(re, im, rows, cos_t, sin_t, inv_hi, inv_lo, last):
    z = wide_dot(jnp.concatenate([re, im], axis=1), inv_hi, inv_lo)
    pieces = []
    for g in range(GRP):
        zr = z[g * FRQ:(g + 1) * FRQ, :BLK]
        zi = z[g * FRQ:(g + 1) * FRQ, BLK:]
        pieces.append(jnp.concatenate([zr * cos_t - zi * sin_t, zr * sin_t + zi * cos_t], axis=0))
    hi, lo = split(jnp.concatenate(pieces, axis=1))
    both = dot(last, hi)
    out = both[:NBLK] + both[NBLK:] + dot(last[:NBLK], lo)
    for g in range(GRP):
        rows[pl.ds(g, NBLK, stride=GRP), :] = out[:, g * BLK:(g + 1) * BLK]
    return rows[...]


def conv_kernel(both, first, cos_t, sin_t, fwd_hi, fwd_lo, inv_hi, inv_lo, last, conv, taps_f, prod_f, rows, work):
    args = (first[...], cos_t[...], sin_t[...], fwd_hi[...], fwd_lo[...])
    taps = to_freq(both[:, :GRP], rows, work, *args)
    taps_f[...] = taps
    prod = to_freq(both[:, GRP:], rows, work, *args)
    prod_f[...] = prod
    tr, ti, pr, pi = taps[:, :BLK], taps[:, BLK:], prod[:, :BLK], prod[:, BLK:]
    out = from_freq(tr * pr - ti * pi, tr * pi + ti * pr, rows, cos_t[...], sin_t[...], inv_hi[...], inv_lo[...], last[...])
    conv[...] = out.astype(BF).reshape(NBLK, GRP, BLK)


def grad_kernel(grad, taps_f, prod_f, first, cos_t, sin_t, fwd_hi, fwd_lo, inv_hi, inv_lo, last, out_ref, rows, work):
    g = to_freq(grad[...], rows, work, first[...], cos_t[...], sin_t[...], fwd_hi[...], fwd_lo[...])
    gr, gi = g[:, :BLK], g[:, BLK:]
    for n, other in enumerate((taps_f, prod_f)):
        r, i = other[:, :BLK], other[:, BLK:]
        out = from_freq(gr * r + gi * i, gi * r - gr * i, rows, cos_t[...], sin_t[...], inv_hi[...], inv_lo[...], last[...])
        if n:
            out = out * (1.0 / math.sqrt(BLK * NBLK))
        out_ref[:, n * GRP:(n + 1) * GRP] = out.astype(BF).reshape(NBLK, GRP, BLK)


def scratch():
    return [pltpu.VMEM((NBLK * GRP, BLK), F32), pltpu.VMEM((GRP * FRQ, 2 * BLK), F32)]


PARAMS = dict(compiler_params=pltpu.CompilerParams(vmem_limit_bytes=32 * 1024 * 1024))


def conv_call(both):
    spec = jax.ShapeDtypeStruct((GRP * FRQ, 2 * BLK), F32)
    return pl.pallas_call(
        conv_kernel,
        out_shape=(jax.ShapeDtypeStruct((NBLK, GRP, BLK), BF), spec, spec),
        scratch_shapes=scratch(), **PARAMS,
    )(both, *tables())


def grad_call(grad, taps_f, prod_f):
    return pl.pallas_call(
        grad_kernel,
        out_shape=jax.ShapeDtypeStruct((NBLK, 2 * GRP, BLK), BF),
        scratch_shapes=scratch(), **PARAMS,
    )(grad, taps_f, prod_f, *tables())


keep_prob = 0.9
SEQ = ("yh", "z", "c")
CH = ("yl", "x")
NZ = 8
NX = 4


def shift_by(axis, size, shift):
    return [(i, (i + shift) % size) for i in range(size)]


def permute(value, axis, size, shift):
    return lax.ppermute(value, axis, shift_by(axis, size, shift))


def f32dot(a, b):
    return jnp.dot(a, b, preferred_element_type=F32)


def to_channels(block):
    return block.T.reshape(NBLK, GRP, BLK)


def body(cotangent, keep_mask, gate_out, gate_in, value_in, filter_taps, out_weight):
    yh, z, c = lax.axis_index("yh"), lax.axis_index("z"), lax.axis_index("c")
    yl, x = lax.axis_index("yl"), lax.axis_index("x")
    scale_back = 1.0 / math.sqrt(BLK * NBLK)
    gate_out32 = gate_out.astype(F32)
    product = (gate_in.astype(F32) * value_in.astype(F32)).astype(BF)
    both = jnp.concatenate([to_channels(filter_taps.astype(BF)), to_channels(product)], axis=1)
    both = lax.all_to_all(both, SEQ, split_axis=0, concat_axis=0, tiled=True)

    weights = [out_weight] + [permute(out_weight, "z", NZ, -s) for s in range(1, NZ)]

    dropped = (cotangent.astype(F32) * keep_mask.astype(F32) / keep_prob).astype(BF)
    chunks = dropped.reshape(BLK, 2, 2, BLK)
    first, second = chunks[:, :, 0].reshape(BLK, 2 * BLK), chunks[:, :, 1].reshape(BLK, 2 * BLK)
    mine = jnp.where(c == 0, first, second)
    theirs = jnp.where(c == 0, second, first)
    pair = jnp.concatenate([mine, permute(theirs, "c", 2, 1)], axis=0)
    near = lax.ppermute(pair, ("yh", "yl"), [(0, 0), (2, 1), (1, 2), (3, 3)])
    far = lax.ppermute(pair, ("yh", "yl"), [(2, 0), (0, 1), (3, 2), (1, 3)])
    quad = jnp.concatenate([near, far], axis=0)
    pieces = [quad] + [permute(quad, "x", NX, -s) for s in range(1, NX)]
    columns = jnp.concatenate(pieces, axis=1)

    stacked = jnp.concatenate(weights, axis=0)
    start = (2 * x - z) % NZ * BLK
    doubled = jnp.concatenate([stacked, stacked], axis=0)
    aligned = lax.dynamic_slice_in_dim(doubled, start, NZ * BLK, axis=0)
    partial = f32dot(columns, aligned)

    partial = partial.reshape(2, 2, BLK, 4 * BLK)
    kept, sent = partial[:, 0], partial[:, 1]
    halves = kept + permute(sent.astype(BF), "c", 2, 1).astype(F32)
    swap = yh != yl
    own = jnp.where(swap, halves[1], halves[0])
    away = jnp.where(swap, halves[0], halves[1])
    grad_mixed = own + permute(away.astype(BF), "yh", 2, 1).astype(F32)

    conv_grad = (grad_mixed * gate_out32).astype(BF)

    conv_f, taps_f, prod_f = conv_call(both)
    conv = lax.all_to_all(conv_f, SEQ, split_axis=0, concat_axis=0, tiled=True).reshape(4 * BLK, BLK).T

    mixed_act = (gate_out32 * conv.astype(F32)).astype(BF)
    mixed_pair = jnp.concatenate([mixed_act, permute(mixed_act, "c", 2, 1)], axis=0)
    other_pair = permute(mixed_pair, "yh", 2, 1)
    mixed = jnp.concatenate([jnp.where(swap, other_pair, mixed_pair), jnp.where(swap, mixed_pair, other_pair)], axis=0)
    grad_w = lax.dot_general(columns, mixed, (((0,), (0,)), ((), ())), preferred_element_type=F32).astype(BF)
    grad_w = jnp.concatenate([grad_w, grad_w], axis=0)
    start_w = (z - 2 * x) % NZ * BLK
    grad_w = lax.dynamic_slice_in_dim(grad_w, start_w, NZ * BLK, axis=0).reshape(NZ, BLK, 4 * BLK)
    total = grad_w[0].astype(F32)
    for s in range(1, NZ):
        total = total + permute(grad_w[s], "z", NZ, s).astype(F32)
    grad_weight = total * scale_back

    grad_chan = lax.all_to_all(to_channels(conv_grad), SEQ, split_axis=0, concat_axis=0, tiled=True)
    outs = grad_call(grad_chan, taps_f, prod_f)
    outs = lax.all_to_all(outs, SEQ, split_axis=0, concat_axis=0, tiled=True)
    back = outs[:, :GRP].reshape(4 * BLK, BLK).T.astype(F32)
    grad_filter = outs[:, GRP:].reshape(4 * BLK, BLK).T.astype(F32)
    grad_gate_out = (grad_mixed * conv.astype(F32)).astype(BF)
    grad_gate_in = (back * value_in.astype(F32)).astype(BF)
    grad_value = (back * gate_in.astype(F32)).astype(BF)
    return (grad_gate_out, grad_gate_in, grad_value, grad_filter, grad_weight)


def solution(mesh):
    fine = Mesh(mesh.devices.reshape(2, NZ, 2, 2, NX), ("yh", "z", "c", "yl", "x"))
    spec = P(SEQ, CH)
    return jax.shard_map(body, mesh=fine, in_specs=(spec,) * 7, out_specs=(spec,) * 5, check_vma=False)
```

time: 391 us -> 160 us (0.41)
  waiting for transfers between devices: 215 us -> 58.9 us
  local copies, waits for them, and re-layouts: 69.5 us -> 6.35 us
  starting transfers between devices: 31.1 us -> 73.5 us
  matrix products: 20.8 us -> 3.87 us
  blocking collectives: 14.9 us -> 0 us
  other arithmetic: 22.1 us -> 8.33 us
  between operations: 14.3 us -> 1.31 us
  Pallas kernels: 0 us -> 5.6 us
    all_gather x2 -> x0, waiting for transfers between devices: 101 us -> none  [the longest x1 91.6 us: body(): lax.all_gather(out_weight, 'seq', axis=0, tiled=True)]
    reduce_scatter x1 -> x0, waiting for transfers between devices: 80.1 us -> none  [body(): lax.psum_scatter(lax.dot_general(columns, mixed_act, (((0,), (0,)), ((),...]
    ppermute x0 -> x24, waiting for transfers between devices: none -> 49.5 us  [the longest x22 49.5 us: permute(): return lax.ppermute(value, axis, shift_by(axis, size, shift))]
    ppermute x0 -> x24, starting transfers between devices: none -> 49.3 us  [the longest x22 44.4 us: permute(): return lax.ppermute(value, axis, shift_by(axis, size, shift))]
    unnamed x49 -> x58, local copies, waits for them, and re-layouts: 37.5 us -> 3.37 us
    all_to_all x5 -> x4, waiting for transfers between devices: 33 us -> 9.4 us  [the longest x1 7.4 us: body(): lax.all_to_all(conv_f, SEQ, split_axis=0, concat_axis=0, tiled=True)]
    dot_general x10 -> x2, matrix products: 20.8 us -> 3.87 us  [the longest x1 2.06 us: f32dot(): return jnp.dot(a, b, preferred_element_type=F32)]
    slice x13 -> x2, local copies, waits for them, and re-layouts: 17.2 us -> 0.84 us  [the longest x1 0.82 us: body(): total = total + permute(grad_w[s], 'z', NZ, s).astype(F32)]
  transfers between devices with their start and end apart: 8 -> 28, of which waited for: 7 -> 16; matrix products, arithmetic and copies ran while one was open for 8% -> 9% of each run, Pallas kernels for 0% -> 4%
where the time goes in v1:
time: 160 us; the launch traced here: 158 us
  starting transfers between devices  73.5 us (46%)
  waiting for transfers between devices  58.9 us (37%)
  other arithmetic  8.33 us (5%)
  local copies, waits for them, and re-layouts  6.35 us (4%)
  Pallas kernels  5.6 us (4%)
  matrix products  3.87 us (2%)
    ppermute x22, waiting for transfers between devices, permute(): return lax.ppermute(value, axis, shift_by(axis, size, shift))  49.5 us
    ppermute x22, starting transfers between devices, permute(): return lax.ppermute(value, axis, shift_by(axis, size, shift))  44.4 us
    all_to_all x1, starting transfers between devices, body(): lax.all_to_all(conv_f, SEQ, split_axis=0, concat_axis=0, tiled=True)  7.72 us
    all_to_all x1, waiting for transfers between devices, body(): lax.all_to_all(conv_f, SEQ, split_axis=0, concat_axis=0, tiled=True)  7.4 us
    all_to_all x1, starting transfers between devices, body(): lax.all_to_all(to_channels(conv_grad), SEQ, split_axis=0, concat_axis=0,...  6.6 us
    all_to_all x1, starting transfers between devices, body(): both = lax.all_to_all(both, SEQ, split_axis=0, concat_axis=0, tiled=True)  5.85 us
    ppermute x1, starting transfers between devices, body(): far = lax.ppermute(pair, ('yh', 'yl'), [(2, 0), (0, 1), (3, 2), (1, 3)])  4.27 us
    all_to_all x1, starting transfers between devices, body(): outs = lax.all_to_all(outs, SEQ, split_axis=0, concat_axis=0, tiled=True)  4 us
  transfers between devices with their start and end apart: 28, of which 16 were waited for; matrix products, arithmetic and copies ran while one was open for 9% of the time, Pallas kernels for 4%

profile of v1, /device:TPU:2, one launch (start us, length us, event | category | flops | bytes accessed | tf_op | source)
XLA Modules:
  0.0 157.8 jit_solution(12980879090840690677)
XLA Ops:
  0.7 5.9 %collective-permute-start.6 = (bf16[128,512]{1,0:T(8,128)(2,1)}, bf16[128,512]{1,0:T(8,128)(2,1)S(1)}, u32[]{:S(2)}, u32[]{:S(2)}) collective-permute-start(bf16[128,512]{1,0:T(8,128)(2,1)} %param.29), channel_id=1, source_target_pairs={{0,112},{16,0},{32,16},{48,32},{64,48},{80,64},{96,80},{112,96},{1... | collective-permute-start | bytes 393224 | tf_op jit(solution)/shard_map/ppermute | solution.py:143
  8.5 5.0 %collective-permute-start.9 = (bf16[128,512]{1,0:T(8,128)(2,1)}, bf16[128,512]{1,0:T(8,128)(2,1)S(1)}, u32[]{:S(2)}, u32[]{:S(2)}) collective-permute-start(bf16[128,512]{1,0:T(8,128)(2,1)} %param.29), channel_id=1, source_target_pairs={{0,64},{16,80},{32,96},{48,112},{64,0},{80,16},{96,32},{112,48},{1... | collective-permute-start | bytes 393224 | tf_op jit(solution)/shard_map/ppermute | solution.py:143
  17.8 5.8 %all-to-all-start = ((bf16[32,32,128]{2,1,0:T(8,128)(2,1)}), bf16[32,32,128]{2,1,0:T(8,128)(2,1)S(1)}, u32[]{:S(2)}, u32[]{:S(2)}) async-start(bf16[32,32,128]{2,1,0:T(8,128)(2,1)} %pad_maximum_fusion.1), calls=%async_computation | async-start | bytes 524288 | tf_op jit(solution)/shard_map/all_to_all | solution.py:161
  23.8 3.7 %collective-permute-start.10 = (bf16[128,512]{1,0:T(8,128)(2,1)S(1)}, bf16[128,512]{1,0:T(8,128)(2,1)S(1)}, u32[]{:S(2)}, u32[]{:S(2)}) collective-permute-start(bf16[128,512]{1,0:T(8,128)(2,1)S(1)} %copy-done.9), channel_id=1, source_target_pairs={{0,48},{16,64},{32,80},{48,96},{64,112},{80,0},{96,16},{112,32},{1... | collective-permute-start | bytes 393224 | tf_op jit(solution)/shard_map/ppermute | solution.py:143
  27.5 2.8 %collective-permute-start.11 = (bf16[128,512]{1,0:T(8,128)(2,1)S(1)}, bf16[128,512]{1,0:T(8,128)(2,1)S(1)}, u32[]{:S(2)}, u32[]{:S(2)}) collective-permute-start(bf16[128,512]{1,0:T(8,128)(2,1)S(1)} %copy-done.9), channel_id=1, source_target_pairs={{0,32},{16,48},{32,64},{48,80},{64,96},{80,112},{96,0},{112,16},{1... | collective-permute-start | bytes 393224 | tf_op jit(solution)/shard_map/ppermute | solution.py:143
  30.9 2.8 %collective-permute-done.8 = bf16[128,512]{1,0:T(8,128)(2,1)S(1)} collective-permute-done((bf16[128,512]{1,0:T(8,128)(2,1)}, bf16[128,512]{1,0:T(8,128)(2,1)S(1)}, u32[]{:S(2)}, u32[]{:S(2)}) %collective-permute-start.8) | collective-permute-done | bytes 131104 | tf_op jit(solution)/shard_map/ppermute | solution.py:143
  34.4 4.3 %collective-permute-start.2 = (bf16[256,256]{0,1:T(8,128)(2,1)S(1)}, bf16[256,256]{0,1:T(8,128)(2,1)S(1)}, u32[]{:S(2)}, u32[]{:S(2)}) collective-permute-start(bf16[256,256]{0,1:T(8,128)(2,1)S(1)} %pad_maximum_fusion.5), channel_id=1, source_target_pairs={{128,0},{0,4},{132,128},{4,132},{129,1},{1,5},{133,129},{5,133},{1... | collective-permute-start | bytes 393224 | tf_op jit(solution)/shard_map/ppermute | solution.py:172
  38.7 5.1 %collective-permute-done.10 = bf16[128,512]{1,0:T(8,128)(2,1)S(1)} collective-permute-done((bf16[128,512]{1,0:T(8,128)(2,1)S(1)}, bf16[128,512]{1,0:T(8,128)(2,1)S(1)}, u32[]{:S(2)}, u32[]{:S(2)}) %collective-permute-start.10) | collective-permute-done | bytes 131104 | tf_op jit(solution)/shard_map/ppermute | solution.py:143
  43.8 3.4 %collective-permute-done.11 = bf16[128,512]{1,0:T(8,128)(2,1)S(1)} collective-permute-done((bf16[128,512]{1,0:T(8,128)(2,1)S(1)}, bf16[128,512]{1,0:T(8,128)(2,1)S(1)}, u32[]{:S(2)}, u32[]{:S(2)}) %collective-permute-start.11) | collective-permute-done | bytes 131104 | tf_op jit(solution)/shard_map/ppermute | solution.py:143
  47.2 3.1 %collective-permute-done.12 = bf16[128,512]{1,0:T(8,128)(2,1)S(1)} collective-permute-done((bf16[128,512]{1,0:T(8,128)(2,1)S(1)}, bf16[128,512]{1,0:T(8,128)(2,1)S(1)}, u32[]{:S(2)}, u32[]{:S(2)}) %collective-permute-start.12) | collective-permute-done | bytes 131104 | tf_op jit(solution)/shard_map/ppermute | solution.py:143
  55.4 4.3 %collective-permute-done.5 = bf16[512,256]{0,1:T(8,128)(2,1)S(1)} collective-permute-done((bf16[512,256]{0,1:T(8,128)(2,1)S(1)}, bf16[512,256]{0,1:T(8,128)(2,1)S(1)}, u32[]{:S(2)}, u32[]{:S(2)}) %collective-permute-start.5) | collective-permute-done | bytes 262176 | tf_op jit(solution)/shard_map/ppermute | solution.py:143
  59.7 3.0 %collective-permute-done.4 = bf16[512,256]{0,1:T(8,128)(2,1)S(1)} collective-permute-done((bf16[512,256]{0,1:T(8,128)(2,1)S(1)}, bf16[512,256]{0,1:T(8,128)(2,1)S(1)}, u32[]{:S(2)}, u32[]{:S(2)}) %collective-permute-start.4) | collective-permute-done | bytes 262176 | tf_op jit(solution)/shard_map/ppermute | solution.py:143
  62.8 3.3 %collective-permute-done.3 = bf16[512,256]{0,1:T(8,128)(2,1)S(1)} collective-permute-done((bf16[512,256]{0,1:T(8,128)(2,1)S(1)}, bf16[512,256]{0,1:T(8,128)(2,1)S(1)}, u32[]{:S(2)}, u32[]{:S(2)}) %collective-permute-start.3) | collective-permute-done | bytes 262176 | tf_op jit(solution)/shard_map/ppermute | solution.py:143
  72.2 7.7 %all-to-all-start.1 = ((bf16[32,16,128]{2,1,0:T(8,128)(2,1)}), bf16[32,16,128]{2,1,0:T(8,128)(2,1)S(1)}, u32[]{:S(2)}, u32[]{:S(2)}) async-start(bf16[32,16,128]{2,1,0:T(8,128)(2,1)} %get-tuple-element.8), calls=%async_computation.1 | async-start | bytes 262144 | tf_op jit(solution)/shard_map/all_to_all | solution.py:194
  81.1 3.4 %collective-permute-start.14 = (bf16[128,512]{1,0:T(8,128)(2,1)S(1)}, bf16[128,512]{1,0:T(8,128)(2,1)S(1)}, u32[]{:S(2)}, u32[]{:S(2)}) collective-permute-start(bf16[128,512]{1,0:T(8,128)(2,1)S(1)} %fusion.14), channel_id=1, source_target_pairs={{0,128},{128,0},{1,129},{129,1},{2,130},{130,2},{3,131},{131,3},{4... | collective-permute-start | bytes 393224 | tf_op jit(solution)/shard_map/ppermute | solution.py:143
  84.5 7.4 %all-to-all-done.1 = bf16[32,16,128]{2,1,0:T(8,128)(2,1)S(1)} async-done(((bf16[32,16,128]{2,1,0:T(8,128)(2,1)}), bf16[32,16,128]{2,1,0:T(8,128)(2,1)S(1)}, u32[]{:S(2)}, u32[]{:S(2)}) %all-to-all-start.1) | async-done | bytes 131104 | tf_op jit(solution)/shard_map/all_to_all | solution.py:194
  95.5 6.6 %all-to-all-start.2 = ((bf16[32,16,128]{2,1,0:T(8,128)(2,1)}), bf16[32,16,128]{2,1,0:T(8,128)(2,1)S(1)}, u32[]{:S(2)}, u32[]{:S(2)}) async-start(bf16[32,16,128]{2,1,0:T(8,128)(2,1)} %bitcast.15), calls=%async_computation.2 | async-start | bytes 262144 | tf_op jit(solution)/shard_map/all_to_all | solution.py:209
  114.1 3.0 %shard_map.255 = bf16[32,32,128]{2,1,0:T(8,128)(2,1)} custom-call(bf16[32,16,128]{2,1,0:T(8,128)(2,1)S(1)} %all-to-all-done.2.grad, f32[640,256]{1,0:T(8,128)S(1)} %get-tuple-element.9.taps_f, f32[640,256]{1,0:T(8,128)S(1)} %get-tuple-element.10.prod_f, bf16[160,32]{1,0:T(8,128)(2,1)S(1)} %copy-done.4, f32[40,128]{1,0:T(8,128)S(1)} %copy-done.5, ...), custom_call_target="tpu_custom_call" | custom-call | tf_op jit(solution)/shard_map/pallas_call | solution.py:124
  117.1 4.0 %all-to-all-start.3 = ((bf16[32,32,128]{2,1,0:T(8,128)(2,1)}), bf16[32,32,128]{2,1,0:T(8,128)(2,1)S(1)}, u32[]{:S(2)}, u32[]{:S(2)}) async-start(bf16[32,32,128]{2,1,0:T(8,128)(2,1)} %shard_map.255), calls=%async_computation.3 | async-start | bytes 524288 | tf_op jit(solution)/shard_map/all_to_all | solution.py:211
  121.1 4.8 %collective-permute-start.21 = (bf16[128,512]{1,0:T(8,128)(2,1)}, bf16[128,512]{1,0:T(8,128)(2,1)S(1)}, u32[]{:S(2)}, u32[]{:S(2)}) collective-permute-start(bf16[128,512]{1,0:T(8,128)(2,1)} %get-tuple-element.13), channel_id=1, source_target_pairs={{0,80},{16,96},{32,112},{48,0},{64,16},{80,32},{96,48},{112,64},{1... | collective-permute-start | bytes 393224 | tf_op jit(solution)/shard_map/ppermute | solution.py:143
  127.3 3.3 %collective-permute-start.19 = (bf16[128,512]{1,0:T(8,128)(2,1)}, bf16[128,512]{1,0:T(8,128)(2,1)S(1)}, u32[]{:S(2)}, u32[]{:S(2)}) collective-permute-start(bf16[128,512]{1,0:T(8,128)(2,1)} %get-tuple-element.15), channel_id=1, source_target_pairs={{0,48},{16,64},{32,80},{48,96},{64,112},{80,0},{96,16},{112,32},{1... | collective-permute-start | bytes 393224 | tf_op jit(solution)/shard_map/ppermute | solution.py:143
  133.0 6.8 %collective-permute-done.21 = bf16[128,512]{1,0:T(8,128)(2,1)S(1)} collective-permute-done((bf16[128,512]{1,0:T(8,128)(2,1)}, bf16[128,512]{1,0:T(8,128)(2,1)S(1)}, u32[]{:S(2)}, u32[]{:S(2)}) %collective-permute-start.21) | collective-permute-done | bytes 131104 | tf_op jit(solution)/shard_map/ppermute | solution.py:143
  141.9 6.1 %collective-permute-done.19 = bf16[128,512]{1,0:T(8,128)(2,1)S(1)} collective-permute-done((bf16[128,512]{1,0:T(8,128)(2,1)}, bf16[128,512]{1,0:T(8,128)(2,1)S(1)}, u32[]{:S(2)}, u32[]{:S(2)}) %collective-permute-start.19) | collective-permute-done | bytes 131104 | tf_op jit(solution)/shard_map/ppermute | solution.py:143
  149.3 4.8 %collective-permute-done.17 = bf16[128,512]{1,0:T(8,128)(2,1)S(1)} collective-permute-done((bf16[128,512]{1,0:T(8,128)(2,1)S(1)}, bf16[128,512]{1,0:T(8,128)(2,1)S(1)}, u32[]{:S(2)}, u32[]{:S(2)}) %collective-permute-start.17) | collective-permute-done | bytes 131104 | tf_op jit(solution)/shard_map/ppermute | solution.py:143
  (121 shorter events, 46.0 us)
Async XLA Ops:
  0.7 26.8 %collective-permute-start.6 = (bf16[128,512]{1,0:T(8,128)(2,1)}, bf16[128,512]{1,0:T(8,128)(2,1)S(1)}, u32[]{:S(2)}, u32[]{:S(2)}) collective-permute-start(bf16[128,512]{1,0:T(8,128)(2,1)} %param.29), channel_id=1, source_target_pairs={{0,112},{16,0},{32,16},{48,32},{64,48},{80,64},{96,80},{112,96},{1... | collective-permute-start | bytes 393224 | tf_op jit(solution)/shard_map/ppermute | solution.py:143
  6.6 23.6 %collective-permute-start.7 = (bf16[128,512]{1,0:T(8,128)(2,1)}, bf16[128,512]{1,0:T(8,128)(2,1)S(1)}, u32[]{:S(2)}, u32[]{:S(2)}) collective-permute-start(bf16[128,512]{1,0:T(8,128)(2,1)} %param.29), channel_id=1, source_target_pairs={{0,96},{16,112},{32,0},{48,16},{64,32},{80,48},{96,64},{112,80},{1... | collective-permute-start | bytes 393224 | tf_op jit(solution)/shard_map/ppermute | solution.py:143
  8.0 25.6 %collective-permute-start.8 = (bf16[128,512]{1,0:T(8,128)(2,1)}, bf16[128,512]{1,0:T(8,128)(2,1)S(1)}, u32[]{:S(2)}, u32[]{:S(2)}) collective-permute-start(bf16[128,512]{1,0:T(8,128)(2,1)} %param.29), channel_id=1, source_target_pairs={{0,80},{16,96},{32,112},{48,0},{64,16},{80,32},{96,48},{112,64},{1... | collective-permute-start | bytes 393224 | tf_op jit(solution)/shard_map/ppermute | solution.py:143
  8.5 25.9 %collective-permute-start.9 = (bf16[128,512]{1,0:T(8,128)(2,1)}, bf16[128,512]{1,0:T(8,128)(2,1)S(1)}, u32[]{:S(2)}, u32[]{:S(2)}) collective-permute-start(bf16[128,512]{1,0:T(8,128)(2,1)} %param.29), channel_id=1, source_target_pairs={{0,64},{16,80},{32,96},{48,112},{64,0},{80,16},{96,32},{112,48},{1... | collective-permute-start | bytes 393224 | tf_op jit(solution)/shard_map/ppermute | solution.py:143
  17.8 51.6 %all-to-all-start = ((bf16[32,32,128]{2,1,0:T(8,128)(2,1)}), bf16[32,32,128]{2,1,0:T(8,128)(2,1)S(1)}, u32[]{:S(2)}, u32[]{:S(2)}) async-start(bf16[32,32,128]{2,1,0:T(8,128)(2,1)} %pad_maximum_fusion.1), calls=%async_computation | async-start | bytes 524288 | tf_op jit(solution)/shard_map/all_to_all | solution.py:161
  23.8 20.0 %collective-permute-start.10 = (bf16[128,512]{1,0:T(8,128)(2,1)S(1)}, bf16[128,512]{1,0:T(8,128)(2,1)S(1)}, u32[]{:S(2)}, u32[]{:S(2)}) collective-permute-start(bf16[128,512]{1,0:T(8,128)(2,1)S(1)} %copy-done.9), channel_id=1, source_target_pairs={{0,48},{16,64},{32,80},{48,96},{64,112},{80,0},{96,16},{112,32},{1... | collective-permute-start | bytes 393224 | tf_op jit(solution)/shard_map/ppermute | solution.py:143
  27.5 19.7 %collective-permute-start.11 = (bf16[128,512]{1,0:T(8,128)(2,1)S(1)}, bf16[128,512]{1,0:T(8,128)(2,1)S(1)}, u32[]{:S(2)}, u32[]{:S(2)}) collective-permute-start(bf16[128,512]{1,0:T(8,128)(2,1)S(1)} %copy-done.9), channel_id=1, source_target_pairs={{0,32},{16,48},{32,64},{48,80},{64,96},{80,112},{96,0},{112,16},{1... | collective-permute-start | bytes 393224 | tf_op jit(solution)/shard_map/ppermute | solution.py:143
  30.2 20.0 %collective-permute-start.12 = (bf16[128,512]{1,0:T(8,128)(2,1)S(1)}, bf16[128,512]{1,0:T(8,128)(2,1)S(1)}, u32[]{:S(2)}, u32[]{:S(2)}) collective-permute-start(bf16[128,512]{1,0:T(8,128)(2,1)S(1)} %copy-done.9), channel_id=1, source_target_pairs={{0,16},{16,32},{32,48},{48,64},{64,80},{80,96},{96,112},{112,0},{1... | collective-permute-start | bytes 393224 | tf_op jit(solution)/shard_map/ppermute | solution.py:143
  33.7 16.7 %collective-permute-start.1 = (bf16[256,256]{0,1:T(8,128)(2,1)S(1)}, bf16[256,256]{0,1:T(8,128)(2,1)S(1)}, u32[]{:S(2)}, u32[]{:S(2)}) collective-permute-start(bf16[256,256]{0,1:T(8,128)(2,1)S(1)} %pad_maximum_fusion.5), channel_id=1, source_target_pairs={{0,0},{128,4},{4,128},{132,132},{1,1},{129,5},{5,129},{133,133},{2... | collective-permute-start | bytes 393224 | tf_op jit(solution)/shard_map/ppermute | solution.py:171
  34.4 16.0 %collective-permute-start.2 = (bf16[256,256]{0,1:T(8,128)(2,1)S(1)}, bf16[256,256]{0,1:T(8,128)(2,1)S(1)}, u32[]{:S(2)}, u32[]{:S(2)}) collective-permute-start(bf16[256,256]{0,1:T(8,128)(2,1)S(1)} %pad_maximum_fusion.5), channel_id=1, source_target_pairs={{128,0},{0,4},{132,128},{4,132},{129,1},{1,5},{133,129},{5,133},{1... | collective-permute-start | bytes 393224 | tf_op jit(solution)/shard_map/ppermute | solution.py:172
  52.0 10.7 %collective-permute-start.4 = (bf16[512,256]{0,1:T(8,128)(2,1)S(1)}, bf16[512,256]{0,1:T(8,128)(2,1)S(1)}, u32[]{:S(2)}, u32[]{:S(2)}) collective-permute-start(bf16[512,256]{0,1:T(8,128)(2,1)S(1)} %constant_dynamic-update-slice_fusion), channel_id=1, source_target_pairs={{0,2},{1,3},{2,0},{3,1},{4,6},{5,7},{6,4},{7,5},{8,10},{9,11},{10,... | collective-permute-start | bytes 786440 | tf_op jit(solution)/shard_map/ppermute | solution.py:143
  53.1 12.9 %collective-permute-start.3 = (bf16[512,256]{0,1:T(8,128)(2,1)S(1)}, bf16[512,256]{0,1:T(8,128)(2,1)S(1)}, u32[]{:S(2)}, u32[]{:S(2)}) collective-permute-start(bf16[512,256]{0,1:T(8,128)(2,1)S(1)} %constant_dynamic-update-slice_fusion), channel_id=1, source_target_pairs={{0,3},{1,0},{2,1},{3,2},{4,7},{5,4},{6,5},{7,6},{8,11},{9,8},{10,9... | collective-permute-start | bytes 786440 | tf_op jit(solution)/shard_map/ppermute | solution.py:143
  69.2 10.7 %collective-permute-start.13 = (bf16[2,128,512]{2,1,0:T(8,128)(2,1)S(1)}, bf16[2,128,512]{2,1,0:T(8,128)(2,1)S(1)}, u32[]{:S(2)}, u32[]{:S(2)}) collective-permute-start(bf16[2,128,512]{2,1,0:T(8,128)(2,1)S(1)} %fusion.12), channel_id=1, source_target_pairs={{0,8},{8,0},{1,9},{9,1},{2,10},{10,2},{3,11},{11,3},{4,12},{12,4},... | collective-permute-start | bytes 786440 | tf_op jit(solution)/shard_map/ppermute | solution.py:143
  72.2 19.7 %all-to-all-start.1 = ((bf16[32,16,128]{2,1,0:T(8,128)(2,1)}), bf16[32,16,128]{2,1,0:T(8,128)(2,1)S(1)}, u32[]{:S(2)}, u32[]{:S(2)}) async-start(bf16[32,16,128]{2,1,0:T(8,128)(2,1)} %get-tuple-element.8), calls=%async_computation.1 | async-start | bytes 262144 | tf_op jit(solution)/shard_map/all_to_all | solution.py:194
  81.1 11.0 %collective-permute-start.14 = (bf16[128,512]{1,0:T(8,128)(2,1)S(1)}, bf16[128,512]{1,0:T(8,128)(2,1)S(1)}, u32[]{:S(2)}, u32[]{:S(2)}) collective-permute-start(bf16[128,512]{1,0:T(8,128)(2,1)S(1)} %fusion.14), channel_id=1, source_target_pairs={{0,128},{128,0},{1,129},{129,1},{2,130},{130,2},{3,131},{131,3},{4... | collective-permute-start | bytes 393224 | tf_op jit(solution)/shard_map/ppermute | solution.py:143
  95.5 18.6 %all-to-all-start.2 = ((bf16[32,16,128]{2,1,0:T(8,128)(2,1)}), bf16[32,16,128]{2,1,0:T(8,128)(2,1)S(1)}, u32[]{:S(2)}, u32[]{:S(2)}) async-start(bf16[32,16,128]{2,1,0:T(8,128)(2,1)} %bitcast.15), calls=%async_computation.2 | async-start | bytes 262144 | tf_op jit(solution)/shard_map/all_to_all | solution.py:209
  108.7 21.9 %collective-permute-start.23 = (bf16[128,512]{1,0:T(8,128)(2,1)}, bf16[128,512]{1,0:T(8,128)(2,1)}, u32[]{:S(2)}, u32[]{:S(2)}) collective-permute-start(bf16[128,512]{1,0:T(8,128)(2,1)} %get-tuple-element.17), channel_id=1, source_target_pairs={{0,112},{16,0},{32,16},{48,32},{64,48},{80,64},{96,80},{112,96},{1... | collective-permute-start | bytes 393224 | tf_op jit(solution)/shard_map/ppermute | solution.py:143
  109.7 22.7 %collective-permute-start.22 = (bf16[128,512]{1,0:T(8,128)(2,1)}, bf16[128,512]{1,0:T(8,128)(2,1)}, u32[]{:S(2)}, u32[]{:S(2)}) collective-permute-start(bf16[128,512]{1,0:T(8,128)(2,1)} %get-tuple-element.12), channel_id=1, source_target_pairs={{0,96},{16,112},{32,0},{48,16},{64,32},{80,48},{96,64},{112,80},{1... | collective-permute-start | bytes 393224 | tf_op jit(solution)/shard_map/ppermute | solution.py:143
  117.1 38.9 %all-to-all-start.3 = ((bf16[32,32,128]{2,1,0:T(8,128)(2,1)}), bf16[32,32,128]{2,1,0:T(8,128)(2,1)S(1)}, u32[]{:S(2)}, u32[]{:S(2)}) async-start(bf16[32,32,128]{2,1,0:T(8,128)(2,1)} %shard_map.255), calls=%async_computation.3 | async-start | bytes 524288 | tf_op jit(solution)/shard_map/all_to_all | solution.py:211
  121.1 18.8 %collective-permute-start.21 = (bf16[128,512]{1,0:T(8,128)(2,1)}, bf16[128,512]{1,0:T(8,128)(2,1)S(1)}, u32[]{:S(2)}, u32[]{:S(2)}) collective-permute-start(bf16[128,512]{1,0:T(8,128)(2,1)} %get-tuple-element.13), channel_id=1, source_target_pairs={{0,80},{16,96},{32,112},{48,0},{64,16},{80,32},{96,48},{112,64},{1... | collective-permute-start | bytes 393224 | tf_op jit(solution)/shard_map/ppermute | solution.py:143
  125.9 15.9 %collective-permute-start.20 = (bf16[128,512]{1,0:T(8,128)(2,1)}, bf16[128,512]{1,0:T(8,128)(2,1)S(1)}, u32[]{:S(2)}, u32[]{:S(2)}) collective-permute-start(bf16[128,512]{1,0:T(8,128)(2,1)} %get-tuple-element.14), channel_id=1, source_target_pairs={{0,64},{16,80},{32,96},{48,112},{64,0},{80,16},{96,32},{112,48},{1... | collective-permute-start | bytes 393224 | tf_op jit(solution)/shard_map/ppermute | solution.py:143
  127.3 20.6 %collective-permute-start.19 = (bf16[128,512]{1,0:T(8,128)(2,1)}, bf16[128,512]{1,0:T(8,128)(2,1)S(1)}, u32[]{:S(2)}, u32[]{:S(2)}) collective-permute-start(bf16[128,512]{1,0:T(8,128)(2,1)} %get-tuple-element.15), channel_id=1, source_target_pairs={{0,48},{16,64},{32,80},{48,96},{64,112},{80,0},{96,16},{112,32},{1... | collective-permute-start | bytes 393224 | tf_op jit(solution)/shard_map/ppermute | solution.py:143
  130.6 18.7 %collective-permute-start.18 = (bf16[128,512]{1,0:T(8,128)(2,1)S(1)}, bf16[128,512]{1,0:T(8,128)(2,1)S(1)}, u32[]{:S(2)}, u32[]{:S(2)}) collective-permute-start(bf16[128,512]{1,0:T(8,128)(2,1)S(1)} %get-tuple-element.16), channel_id=1, source_target_pairs={{0,32},{16,48},{32,64},{48,80},{64,96},{80,112},{96,0},{112,16},{1... | collective-permute-start | bytes 393224 | tf_op jit(solution)/shard_map/ppermute | solution.py:143
  132.5 21.7 %collective-permute-start.17 = (bf16[128,512]{1,0:T(8,128)(2,1)S(1)}, bf16[128,512]{1,0:T(8,128)(2,1)S(1)}, u32[]{:S(2)}, u32[]{:S(2)}) collective-permute-start(bf16[128,512]{1,0:T(8,128)(2,1)S(1)} %get-tuple-element.11), channel_id=1, source_target_pairs={{0,16},{16,32},{32,48},{48,64},{64,80},{80,96},{96,112},{112,0},{1... | collective-permute-start | bytes 393224 | tf_op jit(solution)/shard_map/ppermute | solution.py:143
  (24 other events, 335.7 us)

commit v2 on v1

v2 whole, which is shorter than its diff:
```python
import math

import jax
import jax.numpy as jnp
import ml_dtypes
import numpy as np
from jax import lax
from jax.experimental import pallas as pl
from jax.experimental.pallas import tpu as pltpu
from jax.sharding import Mesh, PartitionSpec as P

BF = jnp.bfloat16
F32 = jnp.float32
SDS = jax.ShapeDtypeStruct
keep_prob = 0.9
BLK = 128
NBLK = 32
GRP = 16
FRQ = 40
LEN = 2 * BLK * NBLK
WID = 4 * BLK
TOK = 8 * BLK
NL = 4
ROOT = 1.0 / math.sqrt(BLK * NBLK)
AXES = ("yh", "zl", "zo", "c", "yl", "x")
SEQ = ("yh", "zl", "zo", "c")
CH = ("yl", "x")
OWNED = [(p // 16) * 16 + (p // 2 % 2) * 8 + (p % 2) * 4 + (p // 4 % 4) for p in range(NBLK)]


def split_np(table):
    hi = table.astype(ml_dtypes.bfloat16)
    return hi, (table - hi.astype(np.float64)).astype(ml_dtypes.bfloat16)


def tables():
    f1 = np.arange(FRQ)[:, None]
    live = (f1 <= NBLK).astype(np.float64)
    k = np.arange(NBLK)[None, :]
    ang = 2 * np.pi * ((f1 * k) % (2 * NBLK)) / (2 * NBLK)
    first = np.concatenate([np.cos(ang) * live, -np.sin(ang) * live], 0)
    weight = np.where((f1 == 0) | (f1 == NBLK), 1.0, 2.0) * live / LEN
    last = np.concatenate([np.cos(ang) * weight, -np.sin(ang) * weight], 0).T
    s = np.arange(BLK)
    turns = 2 * np.pi * (f1 * s[None, :]) / LEN
    ang2 = 2 * np.pi * ((s[:, None] * s[None, :]) % BLK) / BLK
    c, d = np.cos(ang2), np.sin(ang2)
    fwd = np.block([[c, -d], [d, c]])
    inv = np.block([[c, d], [-d, c]])
    parts = [*split_np(fwd), *split_np(inv), *split_np(first), *split_np(last)]
    flat = np.zeros((sum(p.shape[0] for p in parts), 2 * BLK), ml_dtypes.bfloat16)
    at = 0
    for p in parts:
        flat[at:at + p.shape[0], :p.shape[1]] = p
        at += p.shape[0]
    return flat, np.concatenate([np.cos(turns), np.sin(turns)], 0).astype(np.float32)


def dot(a, b):
    return jnp.dot(a, b, preferred_element_type=F32)


def split(x):
    hi = x.astype(BF)
    return hi, (x - hi.astype(F32)).astype(BF)


def wide_dot(x, tab, at):
    hi, lo = split(x)
    hi_tab, lo_tab = tab[at:at + 2 * BLK, :], tab[at + 2 * BLK:at + 4 * BLK, :]
    return dot(hi, hi_tab) + dot(lo, hi_tab) + dot(hi, lo_tab)


def to_freq(rows, work, tab, trig):
    cos_t, sin_t = trig[:FRQ, :], trig[FRQ:, :]
    lanes = jnp.concatenate([rows[pl.ds(g, NBLK, stride=GRP), :] for g in range(GRP)], axis=1).astype(BF)
    both = dot(tab[8 * BLK:8 * BLK + 4 * FRQ, :NBLK], lanes)
    part = both[:2 * FRQ] + both[2 * FRQ:]
    for g in range(GRP):
        re = part[:FRQ, g * BLK:(g + 1) * BLK]
        im = part[FRQ:, g * BLK:(g + 1) * BLK]
        work[g * FRQ:(g + 1) * FRQ, :BLK] = re * cos_t + im * sin_t
        work[g * FRQ:(g + 1) * FRQ, BLK:] = im * cos_t - re * sin_t
    return wide_dot(work[...], tab, 0)


def from_freq(re, im, rows, tab, trig):
    cos_t, sin_t = trig[:FRQ, :], trig[FRQ:, :]
    z = wide_dot(jnp.concatenate([re, im], axis=1), tab, 4 * BLK)
    pieces = []
    for g in range(GRP):
        zr = z[g * FRQ:(g + 1) * FRQ, :BLK]
        zi = z[g * FRQ:(g + 1) * FRQ, BLK:]
        pieces.append(jnp.concatenate([zr * cos_t - zi * sin_t, zr * sin_t + zi * cos_t], axis=0))
    hi, lo = split(jnp.concatenate(pieces, axis=1))
    last = tab[8 * BLK + 4 * FRQ:8 * BLK + 4 * FRQ + 2 * NBLK, :2 * FRQ]
    both = dot(last, hi)
    out = both[:NBLK] + both[NBLK:] + dot(last[:NBLK], lo)
    for g in range(GRP):
        rows[pl.ds(g, NBLK, stride=GRP), :] = out[:, g * BLK:(g + 1) * BLK]
    return rows[...]


def here(axis):
    return lax.axis_index(axis)


def flip(index, bit):
    return 1 - index if bit else index


def block_of(zl, j):
    return flip(here("yl"), j // 4) * 16 + zl * 4 + j % 4


def rows_at(index, count):
    return pl.ds(pl.multiple_of(index * count, count), count)


def to_channels(rows):
    return rows.T.astype(BF).reshape(NBLK, GRP, BLK)


def drop_kernel(cot, mask, keep, send, buf, cot_v, mask_v, sems):
    fetch((cot, mask), (cot_v, mask_v), sems)
    buf[...] = (cot_v[...].astype(F32) * mask_v[...].astype(F32) / keep_prob).astype(BF)
    for z in range(2):
        for out, core in ((keep, 0), (send, 1)):
            q = flip(here("zo"), z) * 2 + flip(here("c"), core)
            out[z] = buf[:, rows_at(q, BLK)]


def fetch(sources, places, sems):
    copies = [pltpu.make_async_copy(a, b, sems.at[n]) for n, (a, b) in enumerate(zip(sources, places))]
    for copy in copies:
        copy.start()
    for copy in copies:
        copy.wait()


def join_kernel(*refs):
    at = 0
    for ref in refs[:-1]:
        refs[-1][at:at + ref.shape[0]] = ref[...]
        at += ref.shape[0]


def pre_kernel(*refs):
    sources = refs[:4]
    both = refs[-6]
    fetch(sources, refs[-5:-1], refs[-1])
    taps, gate_in, value, gate_out = refs[-5:-1]
    for n, block in enumerate((taps[...], gate_in[...].astype(F32) * value[...].astype(F32), gate_out[...].astype(F32))):
        chan = to_channels(block)
        for p in range(NBLK):
            both[p, n * GRP:(n + 1) * GRP] = chan[OWNED[p]]


def conv_kernel(both, tab, trig, conv, taps_f, prod_f, m0, m1, m2, m3, rows, work, act):
    rows[...] = both[:, :GRP].astype(F32).reshape(NBLK * GRP, BLK)
    taps = to_freq(rows, work, tab, trig)
    taps_f[...] = taps
    rows[...] = both[:, GRP:2 * GRP].astype(F32).reshape(NBLK * GRP, BLK)
    prod = to_freq(rows, work, tab, trig)
    prod_f[...] = prod
    tr, ti, pr, pi = taps[:, :BLK], taps[:, BLK:], prod[:, :BLK], prod[:, BLK:]
    out = from_freq(tr * pr - ti * pi, tr * pi + ti * pr, rows, tab, trig).astype(BF)
    conv[...] = out.reshape(NBLK, GRP, BLK)
    act[...] = (both[:, 2 * GRP:].astype(F32).reshape(NBLK * GRP, BLK) * out.astype(F32)).astype(BF)
    for s, m in enumerate((m0, m1, m2, m3)):
        for j in range(8):
            m[:, j * BLK:(j + 1) * BLK] = act[rows_at(block_of((here("zl") + s) % NL, j), GRP), :]


def grad_kernel(g0, g1, g2, g3, both, conv, taps_f, prod_f, tab, trig, out_ref, rows, work):
    for s, g in enumerate((g0, g1, g2, g3)):
        for j in range(8):
            rows[rows_at(block_of((here("zl") + NL - s) % NL, j), GRP), :] = g[:, j * BLK:(j + 1) * BLK].astype(F32)
    mixed = rows[...]
    out_ref[:, 2 * GRP:] = (mixed * conv[...].astype(F32).reshape(NBLK * GRP, BLK)).astype(BF).reshape(NBLK, GRP, BLK)
    rows[...] = (mixed * both[:, 2 * GRP:].astype(F32).reshape(NBLK * GRP, BLK)).astype(BF).astype(F32)
    g = to_freq(rows, work, tab, trig)
    gr, gi = g[:, :BLK], g[:, BLK:]
    for n, other in enumerate((taps_f, prod_f)):
        r, i = other[:, :BLK], other[:, BLK:]
        out = from_freq(gr * r + gi * i, gi * r - gr * i, rows, tab, trig)
        if n:
            out = out * ROOT
        out_ref[:, n * GRP:(n + 1) * GRP] = out.astype(BF).reshape(NBLK, GRP, BLK)


def mm1_kernel(q0, q1, q2, q3, w0, w1, w2, cols, kept, sent, wall, full):
    for n, w in enumerate((w0, w1, w2[:BLK], w2[BLK:])):
        zl = flip(here("zl") // 2, n // 2) * 2 + flip(here("zl") % 2, n % 2)
        wall[rows_at((zl - here("x") + NL) % NL, BLK), :] = w[...]
    for r, q in enumerate((q0, q1, q2, q3)):
        for j in range(8):
            at = j // 4 * 4 + flip(here("zo"), j // 2 % 2) * 2 + flip(here("c"), j % 2)
            cols[rows_at(at, BLK), r * BLK:(r + 1) * BLK] = q[j * BLK:(j + 1) * BLK, :]
    a = cols[...]
    full[...] = lax.dot_general(wall[...], a, (((0,), (1,)), ((), ())), preferred_element_type=F32)
    for r in range(4):
        for out, core in ((kept, 0), (sent, 1)):
            e = flip(here("yh"), r // 2) * 4 + flip(here("zo"), r % 2) * 2 + flip(here("c"), core)
            out[r] = full[rows_at(e, 4 * GRP), :].astype(out.dtype)


def sum1_kernel(kept, got, own, s1, s2, s3):
    own[...] = kept[0] + got[0].astype(F32)
    for r, out in ((1, s1), (2, s2), (3, s3)):
        out[...] = (kept[r] + got[r].astype(F32)).astype(BF)


def sum2_kernel(own, g1, g2, g3, o0, o1, o2, o3, buf):
    buf[...] = (own[...] + g1[...].astype(F32) + g2[...].astype(F32) + g3[...].astype(F32)).astype(BF)
    for s, out in enumerate((o0, o1, o2, o3)):
        out[...] = buf[rows_at((here("zl") + s) % NL, GRP), :]


def mm2_kernel(cols, own, sib, o0, o1, o2, o3, mall, full):
    for core, src in enumerate((own, sib)):
        for r in range(4):
            for s in range(NL):
                b = flip(here("yh"), r // 2) * 16 + flip(here("zo"), r % 2) * 8 + flip(here("c"), core) * 4
                b = b + (here("zl") + NL - s) % NL
                mall[rows_at(b, GRP), :] = src[(r * NL + s) * GRP:(r * NL + s + 1) * GRP, :]
    full[...] = dot(mall[...], cols[...])
    base = here("zl") - here("x") + NL
    for s, out in enumerate((o0, o1, o2, o3)):
        out[...] = full[:, rows_at((base + s) % NL, BLK)].astype(out.dtype)


def sum3_kernel(o0, g1, g2, g3, out):
    total = o0[...] + g1[...].astype(F32) + g2[...].astype(F32) + g3[...].astype(F32)
    out[...] = total.T * ROOT


def post_kernel(outs, gate_in, value_in, ggo, ggi, gv, gf):
    def tokens(n):
        rows = [None] * NBLK
        for p in range(NBLK):
            rows[OWNED[p]] = outs[p, n * GRP:(n + 1) * GRP].astype(F32)
        return jnp.concatenate(rows, axis=0).T

    back = tokens(0)
    ggi[...] = (back * value_in[...].astype(F32)).astype(BF)
    gv[...] = (back * gate_in[...].astype(F32)).astype(BF)
    gf[...] = tokens(1)
    ggo[...] = tokens(2).astype(BF)


def call(kernel, outs, *args, scratch=(), far=0):
    scratch = [pltpu.SemaphoreType.DMA((s,)) if isinstance(s, int) else pltpu.VMEM(*s) for s in scratch]
    specs = [pl.BlockSpec(memory_space=pltpu.HBM if n < far else pltpu.VMEM) for n in range(len(args))]
    return pl.pallas_call(
        kernel, out_shape=outs, in_specs=specs, scratch_shapes=scratch,
        compiler_params=pltpu.CompilerParams(vmem_limit_bytes=LIMIT * 1024 * 1024),
    )(*args)


LIMIT = 32


def flips(value, axes, bits):
    size = NL if axes == ("zl",) else 2 ** len(axes)
    return lax.ppermute(value, axes, [(i, i ^ bits) for i in range(size)])


def turn(value, axis, shift):
    return lax.ppermute(value, axis, [(i, (i + shift) % NL) for i in range(NL)])


def crossing(far, z):
    return [(a * 4 + o * 2 + b, b * 4 + (o ^ z) * 2 + (a ^ far)) for a in range(2) for o in range(2) for b in range(2)]


def exchange(block):
    return lax.all_to_all(block, SEQ, split_axis=0, concat_axis=0, tiled=True)


def body(cotangent, keep_mask, gate_out, gate_in, value_in, filter_taps, out_weight):
    tab, trig = tables()
    small, rows, rows32 = SDS((GRP, TOK), BF), SDS((BLK, WID), BF), SDS((BLK, WID), F32)
    freq = SDS((GRP * FRQ, 2 * BLK), F32)
    conv_scratch = [((NBLK * GRP, BLK), F32), ((GRP * FRQ, 2 * BLK), F32)]
    low = flips(out_weight, ("zl",), 1)
    couple = call(join_kernel, SDS((2 * BLK, WID), BF), out_weight, low)
    weights = [out_weight, low, flips(couple, ("zl",), 2)]
    pairs = SDS((2, BLK, BLK), BF)
    keep, send = call(
        drop_kernel, (pairs, pairs), cotangent, keep_mask, far=2,
        scratch=[((BLK, WID), BF), ((BLK, WID), BF), ((BLK, WID), jnp.int32), 2],
    )
    got = flips(send, ("c",), 1)
    pair = jnp.stack([keep, got], axis=1).reshape(2, 2 * BLK, BLK)
    quad = call(
        join_kernel, SDS((TOK, BLK), BF),
        *[lax.ppermute(pair[z], ("yh", "zo", "yl"), crossing(far, z)) for far in range(2) for z in range(2)])
    pieces = [quad] + [turn(quad, "x", -r) for r in range(1, NL)]
    both = call(
        pre_kernel, SDS((NBLK, 3 * GRP, BLK), BF), filter_taps, gate_in, value_in, gate_out, quad, far=5,
        scratch=[((BLK, WID), F32)] + [((BLK, WID), BF)] * 3 + [4],
    )
    both = exchange(both)

    conv, taps_f, prod_f, *acts = call(
        conv_kernel, (SDS((NBLK, GRP, BLK), BF), freq, freq) + (small,) * 4, both, tab, trig,
        scratch=conv_scratch + [((NBLK * GRP, BLK), BF)],
    )
    cols, kept, sent = call(
        mm1_kernel, (SDS((TOK, WID), BF), SDS((4, 4 * GRP, TOK), F32), SDS((4, 4 * GRP, TOK), BF)),
        *pieces, *weights, scratch=[((WID, WID), BF), ((WID, TOK), F32)],
    )
    arrived = flips(sent, ("c",), 1)
    own, *parts = call(sum1_kernel, (SDS((4 * GRP, TOK), F32),) + (SDS((4 * GRP, TOK), BF),) * 3, kept, arrived)
    parts = [flips(v, ("yh", "zo"), b) for b, v in zip((1, 2, 3), parts)]
    grads = call(sum2_kernel, (small,) * 4, own, *parts, scratch=[((4 * GRP, TOK), BF)])
    grads = [grads[0]] + [turn(grads[s], "zl", s) for s in range(1, NL)]

    acts = [acts[0]] + [turn(acts[s], "zl", s) for s in range(1, NL)]
    act = call(join_kernel, SDS((4 * GRP, TOK), BF), *acts)
    group = call(join_kernel, SDS((WID // 2, TOK), BF), act, *[flips(act, ("yh", "zo"), b) for b in (1, 2, 3)])
    sibling = flips(group, ("c",), 1)
    tall = SDS((WID, BLK), BF)
    sums = call(
        mm2_kernel, (SDS((WID, BLK), F32), tall, tall, tall), cols, group, sibling,
        scratch=[((WID, TOK), BF), ((WID, WID), F32)],
    )
    sums = [sums[0]] + [turn(sums[s], "zl", s) for s in range(1, NL)]
    grad_weight = call(sum3_kernel, rows32, *sums)

    outs = call(
        grad_kernel, SDS((NBLK, 3 * GRP, BLK), BF), *grads, both, conv, taps_f, prod_f, tab, trig, scratch=conv_scratch)
    outs = exchange(outs)
    grad_gate_out, grad_gate_in, grad_value, grad_filter = call(
        post_kernel, (rows, rows, rows, rows32), outs, gate_in, value_in)
    return (grad_gate_out, grad_gate_in, grad_value, grad_filter, grad_weight)


def solution(mesh):
    fine = Mesh(mesh.devices.reshape(2, NL, 2, 2, 2, NL), AXES)
    spec = P(SEQ, CH)
    return jax.shard_map(body, mesh=fine, in_specs=(spec,) * 7, out_specs=(spec,) * 5, check_vma=False)
```

time: 160 us -> 111 us (0.69)
  waiting for transfers between devices: 58.9 us -> 33 us
  starting transfers between devices: 73.5 us -> 63.4 us
  other arithmetic: 8.33 us -> 0.01 us
  Pallas kernels: 5.6 us -> 10.9 us
  local copies, waits for them, and re-layouts: 6.35 us -> 1.92 us
  matrix products: 3.87 us -> 0 us
    ppermute x24 -> x27, waiting for transfers between devices: 49.5 us -> 29.9 us  [the longest x12 13.6 us: turn(): return lax.ppermute(value, axis, [(i, (i + shift) % NL) for i in range(NL)])]
    all_to_all x4 -> x2, starting transfers between devices: 24.2 us -> 7.77 us  [exchange(): return lax.all_to_all(block, SEQ, split_axis=0, concat_axis=0, tiled=True)]
    ppermute x24 -> x27, starting transfers between devices: 49.3 us -> 55.6 us  [the longest x12 29.3 us: turn(): return lax.ppermute(value, axis, [(i, (i + shift) % NL) for i in range(NL)])]
    all_to_all x4 -> x2, waiting for transfers between devices: 9.4 us -> 3.14 us  [exchange(): return lax.all_to_all(block, SEQ, split_axis=0, concat_axis=0, tiled=True)]
    pallas_call x2 -> x14, Pallas kernels: 5.6 us -> 10.9 us  [call(): pl.pallas_call(kernel, out_shape=outs, in_specs=specs, scratch_shapes=scr...]
    dot_general x2 -> x0, matrix products: 3.87 us -> none  [the longest x1 2.06 us: f32dot(): return jnp.dot(a, b, preferred_element_type=F32)]
    concatenate x4 -> x0, other arithmetic: 2.6 us -> none  [the longest x1 1.84 us: body(): grad_w = jnp.concatenate([grad_w, grad_w], axis=0)]
    mul x1 -> x0, other arithmetic: 1.81 us -> none  [body(): grad_weight = total * scale_back]
  transfers between devices with their start and end apart: 28 -> 29, of which waited for: 16 -> 8; matrix products, arithmetic and copies ran while one was open for 9% -> 0% of each run, Pallas kernels for 4% -> 9%
where the time goes in v2:
time: 111 us; the launch traced here: 110 us
  starting transfers between devices  63.4 us (57%)
  waiting for transfers between devices  33 us (30%)
  Pallas kernels  10.9 us (10%)
  local copies, waits for them, and re-layouts  1.92 us (2%)
    ppermute x12, starting transfers between devices, turn(): return lax.ppermute(value, axis, [(i, (i + shift) % NL) for i in range(NL)])  29.3 us
    ppermute x11, starting transfers between devices, flips(): return lax.ppermute(value, axes, [(i, i ^ bits) for i in range(size)])  19.4 us
    ppermute x12, waiting for transfers between devices, turn(): return lax.ppermute(value, axis, [(i, (i + shift) % NL) for i in range(NL)])  13.6 us
    pallas_call x14, Pallas kernels, call(): pl.pallas_call(kernel, out_shape=outs, in_specs=specs, scratch_shapes=scr...  10.9 us
    ppermute x11, waiting for transfers between devices, flips(): return lax.ppermute(value, axes, [(i, i ^ bits) for i in range(size)])  9.66 us
    all_to_all x2, starting transfers between devices, exchange(): return lax.all_to_all(block, SEQ, split_axis=0, concat_axis=0, tiled=True)  7.77 us
    ppermute x4, starting transfers between devices, body(): lax.ppermute(pair[z], ('yh', 'zo', 'yl'), crossing(far, z))  6.95 us
    ppermute x4, waiting for transfers between devices, body(): lax.ppermute(pair[z], ('yh', 'zo', 'yl'), crossing(far, z))  6.66 us
  transfers between devices with their start and end apart: 29, of which 8 were waited for; matrix products, arithmetic and copies ran while one was open for 0% of the time, Pallas kernels for 9%

profile of v2, /device:TPU:2, one launch (start us, length us, event | category | flops | bytes accessed | tf_op | source)
XLA Modules:
  0.0 110.1 jit_solution(14749578066476980597)
XLA Ops:
  2.9 3.4 %collective-permute-start.8 = (bf16[128,512]{1,0:T(8,128)(2,1)S(1)}, bf16[128,512]{1,0:T(8,128)(2,1)S(1)}, u32[]{:S(2)}, u32[]{:S(2)}) collective-permute-start(bf16[128,512]{1,0:T(8,128)(2,1)S(1)} %copy-done.3), channel_id=1, source_target_pairs={{0,32},{32,0},{64,96},{96,64},{1,33},{33,1},{65,97},{97,65},{2,34}... | collective-permute-start | bytes 393224 | tf_op jit(solution)/shard_map/ppermute | solution.py:266
  7.0 2.0 %collective-permute-start.2 = (bf16[256,128]{1,0:T(8,128)(2,1)S(1)}, bf16[256,128]{1,0:T(8,128)(2,1)S(1)}, u32[]{:S(2)}, u32[]{:S(2)}) collective-permute-start(bf16[256,128]{1,0:T(8,128)(2,1)S(1)} %bitcast.5), channel_id=1, source_target_pairs={{0,16},{4,144},{16,0},{20,128},{128,20},{132,148},{144,4},{148,132... | collective-permute-start | bytes 196616 | tf_op jit(solution)/shard_map/ppermute | solution.py:298
  9.0 4.3 %collective-permute-start.3 = (bf16[256,128]{1,0:T(8,128)(2,1)S(1)}, bf16[256,128]{1,0:T(8,128)(2,1)S(1)}, u32[]{:S(2)}, u32[]{:S(2)}) collective-permute-start(bf16[256,128]{1,0:T(8,128)(2,1)S(1)} %bitcast.8), channel_id=1, source_target_pairs={{0,4},{4,132},{16,20},{20,148},{128,0},{132,128},{144,16},{148,144... | collective-permute-start | bytes 196616 | tf_op jit(solution)/shard_map/ppermute | solution.py:298
  13.3 3.8 %collective-permute-done.3.refs_2_ = bf16[256,128]{1,0:T(8,128)(2,1)S(1)} collective-permute-done((bf16[256,128]{1,0:T(8,128)(2,1)S(1)}, bf16[256,128]{1,0:T(8,128)(2,1)S(1)}, u32[]{:S(2)}, u32[]{:S(2)}) %collective-permute-start.3) | collective-permute-done | bytes 65568 | tf_op jit(solution)/shard_map/ppermute | solution.py:298
  17.1 2.8 %collective-permute-done.4.refs_3_ = bf16[256,128]{1,0:T(8,128)(2,1)S(1)} collective-permute-done((bf16[256,128]{1,0:T(8,128)(2,1)S(1)}, bf16[256,128]{1,0:T(8,128)(2,1)S(1)}, u32[]{:S(2)}, u32[]{:S(2)}) %collective-permute-start.4) | collective-permute-done | bytes 65568 | tf_op jit(solution)/shard_map/ppermute | solution.py:298
  20.6 2.4 %collective-permute-start.6 = (bf16[1024,128]{1,0:T(8,128)(2,1)S(1)}, bf16[1024,128]{1,0:T(8,128)(2,1)S(1)}, u32[]{:S(2)}, u32[]{:S(2)}) collective-permute-start(bf16[1024,128]{1,0:T(8,128)(2,1)S(1)} %shard_map.129.q0.refs_4_), channel_id=1, source_target_pairs={{0,2},{1,3},{2,0},{3,1},{4,6},{5,7},{6,4},{7,5},{8,10},{9,11},{10,... | collective-permute-start | bytes 786440 | tf_op jit(solution)/shard_map/ppermute | solution.py:270
  24.8 5.3 %collective-permute-start.9 = (bf16[256,512]{1,0:T(8,128)(2,1)S(1)}, bf16[256,512]{1,0:T(8,128)(2,1)S(1)}, u32[]{:S(2)}, u32[]{:S(2)}) collective-permute-start(bf16[256,512]{1,0:T(8,128)(2,1)S(1)} %shard_map.130), channel_id=1, source_target_pairs={{0,64},{32,96},{64,0},{96,32},{1,65},{33,97},{65,1},{97,33},{2,66}... | collective-permute-start | bytes 786440 | tf_op jit(solution)/shard_map/ppermute | solution.py:266
  31.7 3.9 %all-to-all-start = ((bf16[32,48,128]{2,1,0:T(8,128)(2,1)}), bf16[32,48,128]{2,1,0:T(8,128)(2,1)S(1)}, u32[]{:S(2)}, u32[]{:S(2)}) async-start(bf16[32,48,128]{2,1,0:T(8,128)(2,1)} %shard_map.134), calls=%async_computation | async-start | bytes 786432 | tf_op jit(solution)/shard_map/all_to_all | solution.py:278
  35.6 6.1 %collective-permute-done.9.w2 = bf16[256,512]{1,0:T(8,128)(2,1)S(1)} collective-permute-done((bf16[256,512]{1,0:T(8,128)(2,1)S(1)}, bf16[256,512]{1,0:T(8,128)(2,1)S(1)}, u32[]{:S(2)}, u32[]{:S(2)}) %collective-permute-start.9) | collective-permute-done | bytes 262176 | tf_op jit(solution)/shard_map/ppermute | solution.py:266
  45.0 4.9 %collective-permute-start.13 = (bf16[64,1024]{1,0:T(8,128)(2,1)S(1)}, bf16[64,1024]{1,0:T(8,128)(2,1)S(1)}, u32[]{:S(2)}, u32[]{:S(2)}) collective-permute-start(bf16[64,1024]{1,0:T(8,128)(2,1)S(1)} %get-tuple-element.40), channel_id=1, source_target_pairs={{0,144},{16,128},{128,16},{144,0},{1,145},{17,129},{129,17},{145,1... | collective-permute-start | bytes 393224 | tf_op jit(solution)/shard_map/ppermute | solution.py:266
  49.9 3.1 %all-to-all-done.both = bf16[32,48,128]{2,1,0:T(8,128)(2,1)S(1)} async-done(((bf16[32,48,128]{2,1,0:T(8,128)(2,1)}), bf16[32,48,128]{2,1,0:T(8,128)(2,1)S(1)}, u32[]{:S(2)}, u32[]{:S(2)}) %all-to-all-start) | async-done | bytes 393248 | tf_op jit(solution)/shard_map/all_to_all | solution.py:278
  53.0 2.0 %shard_map.135 = (bf16[32,16,128]{2,1,0:T(8,128)(2,1)S(1)}, f32[640,256]{1,0:T(8,128)S(1)}, f32[640,256]{1,0:T(8,128)S(1)}, bf16[16,1024]{1,0:T(8,128)(2,1)S(1)}...) custom-call(bf16[32,48,128]{2,1,0:T(8,128)(2,1)S(1)} %all-to-all-done.both, ...), custom_call_target="tpu_custom_call" | custom-call | tf_op jit(solution)/shard_map/pallas_call | solution.py:255
  55.3 2.2 %collective-permute-start.18 = (bf16[16,1024]{1,0:T(8,128)(2,1)S(1)}, bf16[16,1024]{1,0:T(8,128)(2,1)S(1)}, u32[]{:S(2)}, u32[]{:S(2)}) collective-permute-start(bf16[16,1024]{1,0:T(8,128)(2,1)S(1)} %get-tuple-element.55), channel_id=1, source_target_pairs={{0,64},{32,96},{64,0},{96,32},{1,65},{33,97},{65,1},{97,33},{2,66}... | collective-permute-start | bytes 98312 | tf_op jit(solution)/shard_map/ppermute | solution.py:270
  57.5 3.3 %collective-permute-start.19 = (bf16[16,1024]{1,0:T(8,128)(2,1)S(1)}, bf16[16,1024]{1,0:T(8,128)(2,1)S(1)}, u32[]{:S(2)}, u32[]{:S(2)}) collective-permute-start(bf16[16,1024]{1,0:T(8,128)(2,1)S(1)} %get-tuple-element.56), channel_id=1, source_target_pairs={{0,96},{32,0},{64,32},{96,64},{1,97},{33,1},{65,33},{97,65},{2,98}... | collective-permute-start | bytes 98312 | tf_op jit(solution)/shard_map/ppermute | solution.py:270
  62.0 3.7 %collective-permute-start.15 = (bf16[16,1024]{1,0:T(8,128)(2,1)S(1)}, bf16[16,1024]{1,0:T(8,128)(2,1)S(1)}, u32[]{:S(2)}, u32[]{:S(2)}) collective-permute-start(bf16[16,1024]{1,0:T(8,128)(2,1)S(1)} %get-tuple-element.43), channel_id=1, source_target_pairs={{0,64},{32,96},{64,0},{96,32},{1,65},{33,97},{65,1},{97,33},{2,66}... | collective-permute-start | bytes 98312 | tf_op jit(solution)/shard_map/ppermute | solution.py:270
  65.6 4.0 %collective-permute-start.16 = (bf16[16,1024]{1,0:T(8,128)(2,1)S(1)}, bf16[16,1024]{1,0:T(8,128)(2,1)S(1)}, u32[]{:S(2)}, u32[]{:S(2)}) collective-permute-start(bf16[16,1024]{1,0:T(8,128)(2,1)S(1)} %get-tuple-element.44), channel_id=1, source_target_pairs={{0,96},{32,0},{64,32},{96,64},{1,97},{33,1},{65,33},{97,65},{2,98}... | collective-permute-start | bytes 98312 | tf_op jit(solution)/shard_map/ppermute | solution.py:270
  72.4 2.3 %collective-permute-start.22 = (bf16[64,1024]{1,0:T(8,128)(2,1)S(1)}, bf16[64,1024]{1,0:T(8,128)(2,1)S(1)}, u32[]{:S(2)}, u32[]{:S(2)}) collective-permute-start(bf16[64,1024]{1,0:T(8,128)(2,1)S(1)} %shard_map.138.refs_0_), channel_id=1, source_target_pairs={{0,144},{16,128},{128,16},{144,0},{1,145},{17,129},{129,17},{145,1... | collective-permute-start | bytes 393224 | tf_op jit(solution)/shard_map/ppermute | solution.py:266
  74.8 3.2 %shard_map.136 = bf16[32,48,128]{2,1,0:T(8,128)(2,1)} custom-call(bf16[16,1024]{1,0:T(8,128)(2,1)S(1)} %get-tuple-element.41.g0, bf16[16,1024]{1,0:T(8,128)(2,1)S(1)} %collective-permute-done.14.g1, bf16[16,1024]{1,0:T(8,128)(2,1)S(1)} %collective-permute-done.15.g2, bf16[16,1024]{1,0:T(8,128)(2,1)S(1)} %collective-permute-done.16.g3, ...), custom_call_target="tpu_custom_call" | custom-call | tf_op jit(solution)/shard_map/pallas_call | solution.py:255
  78.0 3.9 %all-to-all-start.1 = ((bf16[32,48,128]{2,1,0:T(8,128)(2,1)}), bf16[32,48,128]{2,1,0:T(8,128)(2,1)S(1)}, u32[]{:S(2)}, u32[]{:S(2)}) async-start(bf16[32,48,128]{2,1,0:T(8,128)(2,1)} %shard_map.136), calls=%async_computation.1 | async-start | bytes 786432 | tf_op jit(solution)/shard_map/all_to_all | solution.py:278
  84.9 2.7 %collective-permute-start.24 = (bf16[512,128]{1,0:T(8,128)(2,1)S(1)}, bf16[512,128]{1,0:T(8,128)(2,1)S(1)}, u32[]{:S(2)}, u32[]{:S(2)}) collective-permute-start(bf16[512,128]{1,0:T(8,128)(2,1)S(1)} %get-tuple-element.58), channel_id=1, source_target_pairs={{0,32},{32,64},{64,96},{96,0},{1,33},{33,65},{65,97},{97,1},{2,34}... | collective-permute-start | bytes 393224 | tf_op jit(solution)/shard_map/ppermute | solution.py:270
  87.6 3.6 %collective-permute-start.25 = (bf16[512,128]{1,0:T(8,128)(2,1)S(1)}, bf16[512,128]{1,0:T(8,128)(2,1)S(1)}, u32[]{:S(2)}, u32[]{:S(2)}) collective-permute-start(bf16[512,128]{1,0:T(8,128)(2,1)S(1)} %get-tuple-element.59), channel_id=1, source_target_pairs={{0,64},{32,96},{64,0},{96,32},{1,65},{33,97},{65,1},{97,33},{2,66}... | collective-permute-start | bytes 393224 | tf_op jit(solution)/shard_map/ppermute | solution.py:270
  91.2 3.6 %collective-permute-start.26 = (bf16[512,128]{1,0:T(8,128)(2,1)S(1)}, bf16[512,128]{1,0:T(8,128)(2,1)S(1)}, u32[]{:S(2)}, u32[]{:S(2)}) collective-permute-start(bf16[512,128]{1,0:T(8,128)(2,1)S(1)} %get-tuple-element.60), channel_id=1, source_target_pairs={{0,96},{32,0},{64,32},{96,64},{1,97},{33,1},{65,33},{97,65},{2,98}... | collective-permute-start | bytes 393224 | tf_op jit(solution)/shard_map/ppermute | solution.py:270
  94.7 5.6 %collective-permute-done.24.g1 = bf16[512,128]{1,0:T(8,128)(2,1)S(1)} collective-permute-done((bf16[512,128]{1,0:T(8,128)(2,1)S(1)}, bf16[512,128]{1,0:T(8,128)(2,1)S(1)}, u32[]{:S(2)}, u32[]{:S(2)}) %collective-permute-start.24) | collective-permute-done | bytes 131104 | tf_op jit(solution)/shard_map/ppermute | solution.py:270
  100.4 7.9 %collective-permute-done.25.g2 = bf16[512,128]{1,0:T(8,128)(2,1)S(1)} collective-permute-done((bf16[512,128]{1,0:T(8,128)(2,1)S(1)}, bf16[512,128]{1,0:T(8,128)(2,1)S(1)}, u32[]{:S(2)}, u32[]{:S(2)}) %collective-permute-start.25) | collective-permute-done | bytes 131104 | tf_op jit(solution)/shard_map/ppermute | solution.py:270
  (67 shorter events, 19.1 us)
Async XLA Ops:
  2.9 21.9 %collective-permute-start.8 = (bf16[128,512]{1,0:T(8,128)(2,1)S(1)}, bf16[128,512]{1,0:T(8,128)(2,1)S(1)}, u32[]{:S(2)}, u32[]{:S(2)}) collective-permute-start(bf16[128,512]{1,0:T(8,128)(2,1)S(1)} %copy-done.3), channel_id=1, source_target_pairs={{0,32},{32,0},{64,96},{96,64},{1,33},{33,1},{65,97},{97,65},{2,34}... | collective-permute-start | bytes 393224 | tf_op jit(solution)/shard_map/ppermute | solution.py:266
  6.3 7.0 %collective-permute-start.1 = (bf16[256,128]{1,0:T(8,128)(2,1)S(1)}, bf16[256,128]{1,0:T(8,128)(2,1)S(1)}, u32[]{:S(2)}, u32[]{:S(2)}) collective-permute-start(bf16[256,128]{1,0:T(8,128)(2,1)S(1)} %bitcast.7), channel_id=1, source_target_pairs={{0,0},{4,128},{16,16},{20,144},{128,4},{132,132},{144,20},{148,148... | collective-permute-start | bytes 196616 | tf_op jit(solution)/shard_map/ppermute | solution.py:298
  9.0 8.1 %collective-permute-start.3 = (bf16[256,128]{1,0:T(8,128)(2,1)S(1)}, bf16[256,128]{1,0:T(8,128)(2,1)S(1)}, u32[]{:S(2)}, u32[]{:S(2)}) collective-permute-start(bf16[256,128]{1,0:T(8,128)(2,1)S(1)} %bitcast.8), channel_id=1, source_target_pairs={{0,4},{4,132},{16,20},{20,148},{128,0},{132,128},{144,16},{148,144... | collective-permute-start | bytes 196616 | tf_op jit(solution)/shard_map/ppermute | solution.py:298
  20.0 15.6 %collective-permute-start.5 = (bf16[1024,128]{1,0:T(8,128)(2,1)S(1)}, bf16[1024,128]{1,0:T(8,128)(2,1)S(1)}, u32[]{:S(2)}, u32[]{:S(2)}) collective-permute-start(bf16[1024,128]{1,0:T(8,128)(2,1)S(1)} %shard_map.129.q0.refs_4_), channel_id=1, source_target_pairs={{0,3},{1,0},{2,1},{3,2},{4,7},{5,4},{6,5},{7,6},{8,11},{9,8},{10,9... | collective-permute-start | bytes 786440 | tf_op jit(solution)/shard_map/ppermute | solution.py:270
  20.6 15.0 %collective-permute-start.6 = (bf16[1024,128]{1,0:T(8,128)(2,1)S(1)}, bf16[1024,128]{1,0:T(8,128)(2,1)S(1)}, u32[]{:S(2)}, u32[]{:S(2)}) collective-permute-start(bf16[1024,128]{1,0:T(8,128)(2,1)S(1)} %shard_map.129.q0.refs_4_), channel_id=1, source_target_pairs={{0,2},{1,3},{2,0},{3,1},{4,6},{5,7},{6,4},{7,5},{8,10},{9,11},{10,... | collective-permute-start | bytes 786440 | tf_op jit(solution)/shard_map/ppermute | solution.py:270
  23.0 12.6 %collective-permute-start.7 = (bf16[1024,128]{1,0:T(8,128)(2,1)S(1)}, bf16[1024,128]{1,0:T(8,128)(2,1)S(1)}, u32[]{:S(2)}, u32[]{:S(2)}) collective-permute-start(bf16[1024,128]{1,0:T(8,128)(2,1)S(1)} %shard_map.129.q0.refs_4_), channel_id=1, source_target_pairs={{0,1},{1,2},{2,3},{3,0},{4,5},{5,6},{6,7},{7,4},{8,9},{9,10},{10,1... | collective-permute-start | bytes 786440 | tf_op jit(solution)/shard_map/ppermute | solution.py:270
  24.8 16.9 %collective-permute-start.9 = (bf16[256,512]{1,0:T(8,128)(2,1)S(1)}, bf16[256,512]{1,0:T(8,128)(2,1)S(1)}, u32[]{:S(2)}, u32[]{:S(2)}) collective-permute-start(bf16[256,512]{1,0:T(8,128)(2,1)S(1)} %shard_map.130), channel_id=1, source_target_pairs={{0,64},{32,96},{64,0},{96,32},{1,65},{33,97},{65,1},{97,33},{2,66}... | collective-permute-start | bytes 786440 | tf_op jit(solution)/shard_map/ppermute | solution.py:266
  31.7 21.4 %all-to-all-start = ((bf16[32,48,128]{2,1,0:T(8,128)(2,1)}), bf16[32,48,128]{2,1,0:T(8,128)(2,1)S(1)}, u32[]{:S(2)}, u32[]{:S(2)}) async-start(bf16[32,48,128]{2,1,0:T(8,128)(2,1)} %shard_map.134), calls=%async_computation | async-start | bytes 786432 | tf_op jit(solution)/shard_map/all_to_all | solution.py:278
  44.8 12.7 %collective-permute-start.11 = (bf16[64,1024]{1,0:T(8,128)(2,1)S(1)}, bf16[64,1024]{1,0:T(8,128)(2,1)S(1)}, u32[]{:S(2)}, u32[]{:S(2)}) collective-permute-start(bf16[64,1024]{1,0:T(8,128)(2,1)S(1)} %get-tuple-element.38), channel_id=1, source_target_pairs={{0,16},{16,0},{128,144},{144,128},{1,17},{17,1},{129,145},{145,129... | collective-permute-start | bytes 393224 | tf_op jit(solution)/shard_map/ppermute | solution.py:266
  44.9 15.9 %collective-permute-start.12 = (bf16[64,1024]{1,0:T(8,128)(2,1)S(1)}, bf16[64,1024]{1,0:T(8,128)(2,1)S(1)}, u32[]{:S(2)}, u32[]{:S(2)}) collective-permute-start(bf16[64,1024]{1,0:T(8,128)(2,1)S(1)} %get-tuple-element.39), channel_id=1, source_target_pairs={{0,128},{16,144},{128,0},{144,16},{1,129},{17,145},{129,1},{145,17... | collective-permute-start | bytes 393224 | tf_op jit(solution)/shard_map/ppermute | solution.py:266
  45.0 15.8 %collective-permute-start.13 = (bf16[64,1024]{1,0:T(8,128)(2,1)S(1)}, bf16[64,1024]{1,0:T(8,128)(2,1)S(1)}, u32[]{:S(2)}, u32[]{:S(2)}) collective-permute-start(bf16[64,1024]{1,0:T(8,128)(2,1)S(1)} %get-tuple-element.40), channel_id=1, source_target_pairs={{0,144},{16,128},{128,16},{144,0},{1,145},{17,129},{129,17},{145,1... | collective-permute-start | bytes 393224 | tf_op jit(solution)/shard_map/ppermute | solution.py:266
  55.0 10.6 %collective-permute-start.17 = (bf16[16,1024]{1,0:T(8,128)(2,1)S(1)}, bf16[16,1024]{1,0:T(8,128)(2,1)S(1)}, u32[]{:S(2)}, u32[]{:S(2)}) collective-permute-start(bf16[16,1024]{1,0:T(8,128)(2,1)S(1)} %get-tuple-element.54), channel_id=1, source_target_pairs={{0,32},{32,64},{64,96},{96,0},{1,33},{33,65},{65,97},{97,1},{2,34}... | collective-permute-start | bytes 98312 | tf_op jit(solution)/shard_map/ppermute | solution.py:270
  55.3 14.3 %collective-permute-start.18 = (bf16[16,1024]{1,0:T(8,128)(2,1)S(1)}, bf16[16,1024]{1,0:T(8,128)(2,1)S(1)}, u32[]{:S(2)}, u32[]{:S(2)}) collective-permute-start(bf16[16,1024]{1,0:T(8,128)(2,1)S(1)} %get-tuple-element.55), channel_id=1, source_target_pairs={{0,64},{32,96},{64,0},{96,32},{1,65},{33,97},{65,1},{97,33},{2,66}... | collective-permute-start | bytes 98312 | tf_op jit(solution)/shard_map/ppermute | solution.py:270
  57.5 12.2 %collective-permute-start.19 = (bf16[16,1024]{1,0:T(8,128)(2,1)S(1)}, bf16[16,1024]{1,0:T(8,128)(2,1)S(1)}, u32[]{:S(2)}, u32[]{:S(2)}) collective-permute-start(bf16[16,1024]{1,0:T(8,128)(2,1)S(1)} %get-tuple-element.56), channel_id=1, source_target_pairs={{0,96},{32,0},{64,32},{96,64},{1,97},{33,1},{65,33},{97,65},{2,98}... | collective-permute-start | bytes 98312 | tf_op jit(solution)/shard_map/ppermute | solution.py:270
  60.9 11.5 %collective-permute-start.14 = (bf16[16,1024]{1,0:T(8,128)(2,1)S(1)}, bf16[16,1024]{1,0:T(8,128)(2,1)S(1)}, u32[]{:S(2)}, u32[]{:S(2)}) collective-permute-start(bf16[16,1024]{1,0:T(8,128)(2,1)S(1)} %get-tuple-element.42), channel_id=1, source_target_pairs={{0,32},{32,64},{64,96},{96,0},{1,33},{33,65},{65,97},{97,1},{2,34}... | collective-permute-start | bytes 98312 | tf_op jit(solution)/shard_map/ppermute | solution.py:270
  62.0 12.8 %collective-permute-start.15 = (bf16[16,1024]{1,0:T(8,128)(2,1)S(1)}, bf16[16,1024]{1,0:T(8,128)(2,1)S(1)}, u32[]{:S(2)}, u32[]{:S(2)}) collective-permute-start(bf16[16,1024]{1,0:T(8,128)(2,1)S(1)} %get-tuple-element.43), channel_id=1, source_target_pairs={{0,64},{32,96},{64,0},{96,32},{1,65},{33,97},{65,1},{97,33},{2,66}... | collective-permute-start | bytes 98312 | tf_op jit(solution)/shard_map/ppermute | solution.py:270
  65.6 9.1 %collective-permute-start.16 = (bf16[16,1024]{1,0:T(8,128)(2,1)S(1)}, bf16[16,1024]{1,0:T(8,128)(2,1)S(1)}, u32[]{:S(2)}, u32[]{:S(2)}) collective-permute-start(bf16[16,1024]{1,0:T(8,128)(2,1)S(1)} %get-tuple-element.44), channel_id=1, source_target_pairs={{0,96},{32,0},{64,32},{96,64},{1,97},{33,1},{65,33},{97,65},{2,98}... | collective-permute-start | bytes 98312 | tf_op jit(solution)/shard_map/ppermute | solution.py:270
  69.7 12.2 %collective-permute-start.20 = (bf16[64,1024]{1,0:T(8,128)(2,1)S(1)}, bf16[64,1024]{1,0:T(8,128)(2,1)S(1)}, u32[]{:S(2)}, u32[]{:S(2)}) collective-permute-start(bf16[64,1024]{1,0:T(8,128)(2,1)S(1)} %shard_map.138.refs_0_), channel_id=1, source_target_pairs={{0,16},{16,0},{128,144},{144,128},{1,17},{17,1},{129,145},{145,129... | collective-permute-start | bytes 393224 | tf_op jit(solution)/shard_map/ppermute | solution.py:266
  70.6 11.3 %collective-permute-start.21 = (bf16[64,1024]{1,0:T(8,128)(2,1)S(1)}, bf16[64,1024]{1,0:T(8,128)(2,1)S(1)}, u32[]{:S(2)}, u32[]{:S(2)}) collective-permute-start(bf16[64,1024]{1,0:T(8,128)(2,1)S(1)} %shard_map.138.refs_0_), channel_id=1, source_target_pairs={{0,128},{16,144},{128,0},{144,16},{1,129},{17,145},{129,1},{145,17... | collective-permute-start | bytes 393224 | tf_op jit(solution)/shard_map/ppermute | solution.py:266
  72.4 9.5 %collective-permute-start.22 = (bf16[64,1024]{1,0:T(8,128)(2,1)S(1)}, bf16[64,1024]{1,0:T(8,128)(2,1)S(1)}, u32[]{:S(2)}, u32[]{:S(2)}) collective-permute-start(bf16[64,1024]{1,0:T(8,128)(2,1)S(1)} %shard_map.138.refs_0_), channel_id=1, source_target_pairs={{0,144},{16,128},{128,16},{144,0},{1,145},{17,129},{129,17},{145,1... | collective-permute-start | bytes 393224 | tf_op jit(solution)/shard_map/ppermute | solution.py:266
  78.0 31.2 %all-to-all-start.1 = ((bf16[32,48,128]{2,1,0:T(8,128)(2,1)}), bf16[32,48,128]{2,1,0:T(8,128)(2,1)S(1)}, u32[]{:S(2)}, u32[]{:S(2)}) async-start(bf16[32,48,128]{2,1,0:T(8,128)(2,1)} %shard_map.136), calls=%async_computation.1 | async-start | bytes 786432 | tf_op jit(solution)/shard_map/all_to_all | solution.py:278
  84.9 15.5 %collective-permute-start.24 = (bf16[512,128]{1,0:T(8,128)(2,1)S(1)}, bf16[512,128]{1,0:T(8,128)(2,1)S(1)}, u32[]{:S(2)}, u32[]{:S(2)}) collective-permute-start(bf16[512,128]{1,0:T(8,128)(2,1)S(1)} %get-tuple-element.58), channel_id=1, source_target_pairs={{0,32},{32,64},{64,96},{96,0},{1,33},{33,65},{65,97},{97,1},{2,34}... | collective-permute-start | bytes 393224 | tf_op jit(solution)/shard_map/ppermute | solution.py:270
  87.6 20.7 %collective-permute-start.25 = (bf16[512,128]{1,0:T(8,128)(2,1)S(1)}, bf16[512,128]{1,0:T(8,128)(2,1)S(1)}, u32[]{:S(2)}, u32[]{:S(2)}) collective-permute-start(bf16[512,128]{1,0:T(8,128)(2,1)S(1)} %get-tuple-element.59), channel_id=1, source_target_pairs={{0,64},{32,96},{64,0},{96,32},{1,65},{33,97},{65,1},{97,33},{2,66}... | collective-permute-start | bytes 393224 | tf_op jit(solution)/shard_map/ppermute | solution.py:270
  91.2 17.1 %collective-permute-start.26 = (bf16[512,128]{1,0:T(8,128)(2,1)S(1)}, bf16[512,128]{1,0:T(8,128)(2,1)S(1)}, u32[]{:S(2)}, u32[]{:S(2)}) collective-permute-start(bf16[512,128]{1,0:T(8,128)(2,1)S(1)} %get-tuple-element.60), channel_id=1, source_target_pairs={{0,96},{32,0},{64,32},{96,64},{1,97},{33,1},{65,33},{97,65},{2,98}... | collective-permute-start | bytes 393224 | tf_op jit(solution)/shard_map/ppermute | solution.py:270
  (14 other events, 82.2 us)

commit v3 on v2

--- a/solution.py
+++ b/solution.py
@@ -145,6 +145,11 @@
         at += ref.shape[0]
 
 
+def half_kernel(*refs):
+    for n, ref in enumerate(refs[:-1]):
+        refs[-1][n * GRP:(n + 1) * GRP] = ref[GRP:]
+
+
 def pre_kernel(*refs):
     sources = refs[:4]
     both = refs[-6]
@@ -175,7 +180,7 @@
 def grad_kernel(g0, g1, g2, g3, both, conv, taps_f, prod_f, tab, trig, out_ref, rows, work):
     for s, g in enumerate((g0, g1, g2, g3)):
         for j in range(8):
-            rows[rows_at(block_of((here("zl") + NL - s) % NL, j), GRP), :] = g[:, j * BLK:(j + 1) * BLK].astype(F32)
+            rows[rows_at(block_of((here("zl") + NL - s) % NL, j), GRP), :] = g[:GRP, j * BLK:(j + 1) * BLK].astype(F32)
     mixed = rows[...]
     out_ref[:, 2 * GRP:] = (mixed * conv[...].astype(F32).reshape(NBLK * GRP, BLK)).astype(BF).reshape(NBLK, GRP, BLK)
     rows[...] = (mixed * both[:, 2 * GRP:].astype(F32).reshape(NBLK * GRP, BLK)).astype(BF).astype(F32)
@@ -211,10 +216,11 @@
         out[...] = (kept[r] + got[r].astype(F32)).astype(BF)
 
 
-def sum2_kernel(own, g1, g2, g3, o0, o1, o2, o3, buf):
+def sum2_kernel(own, g1, g2, g3, m0, m1, m2, m3, o0, o1, o2, o3, buf):
     buf[...] = (own[...] + g1[...].astype(F32) + g2[...].astype(F32) + g3[...].astype(F32)).astype(BF)
-    for s, out in enumerate((o0, o1, o2, o3)):
-        out[...] = buf[rows_at((here("zl") + s) % NL, GRP), :]
+    for s, (out, m) in enumerate(((o0, m0), (o1, m1), (o2, m2), (o3, m3))):
+        out[:GRP] = buf[rows_at((here("zl") + s) % NL, GRP), :]
+        out[GRP:] = m[...]
 
 
 def mm2_kernel(cols, own, sib, o0, o1, o2, o3, mall, full):
@@ -258,7 +264,7 @@
     )(*args)
 
 
-LIMIT = 32
+LIMIT = 44
 
 
 def flips(value, axes, bits):
@@ -314,11 +320,10 @@
     arrived = flips(sent, ("c",), 1)
     own, *parts = call(sum1_kernel, (SDS((4 * GRP, TOK), F32),) + (SDS((4 * GRP, TOK), BF),) * 3, kept, arrived)
     parts = [flips(v, ("yh", "zo"), b) for b, v in zip((1, 2, 3), parts)]
-    grads = call(sum2_kernel, (small,) * 4, own, *parts, scratch=[((4 * GRP, TOK), BF)])
+    grads = call(sum2_kernel, (SDS((2 * GRP, TOK), BF),) * 4, own, *parts, *acts, scratch=[((4 * GRP, TOK), BF)])
     grads = [grads[0]] + [turn(grads[s], "zl", s) for s in range(1, NL)]
 
-    acts = [acts[0]] + [turn(acts[s], "zl", s) for s in range(1, NL)]
-    act = call(join_kernel, SDS((4 * GRP, TOK), BF), *acts)
+    act = call(half_kernel, SDS((4 * GRP, TOK), BF), *grads)
     group = call(join_kernel, SDS((WID // 2, TOK), BF), act, *[flips(act, ("yh", "zo"), b) for b in (1, 2, 3)])
     sibling = flips(group, ("c",), 1)
     tall = SDS((WID, BLK), BF)

time: 111 us -> 111 us (level)
  waiting for transfers between devices: 33 us -> 37.2 us
  starting transfers between devices: 63.4 us -> 59.3 us
    ppermute x12 -> x9, starting transfers between devices: 29.3 us -> 23.1 us  [turn(): return lax.ppermute(value, axis, [(i, (i + shift) % NL) for i in range(NL)])]
    all_to_all x2, waiting for transfers between devices: 3.14 us -> 7.4 us  [exchange(): return lax.all_to_all(block, SEQ, split_axis=0, concat_axis=0, tiled=True)]
    all_to_all x2, starting transfers between devices: 7.77 us -> 9.88 us  [exchange(): return lax.all_to_all(block, SEQ, split_axis=0, concat_axis=0, tiled=True)]
    ppermute x12 -> x9, waiting for transfers between devices: 13.6 us -> 13.1 us  [turn(): return lax.ppermute(value, axis, [(i, (i + shift) % NL) for i in range(NL)])]
  transfers between devices with their start and end apart: 29 -> 26, of which waited for: 8 -> 12; matrix products, arithmetic and copies ran while one was open for 0% -> 0% of each run, Pallas kernels for 9% -> 9%
where the time goes in v3:
time: 111 us; the launch traced here: 110 us
  starting transfers between devices  59.3 us (53%)
  waiting for transfers between devices  37.2 us (34%)
  Pallas kernels  10.9 us (10%)
  local copies, waits for them, and re-layouts  1.92 us (2%)
    ppermute x9, starting transfers between devices, turn(): return lax.ppermute(value, axis, [(i, (i + shift) % NL) for i in range(NL)])  23.1 us
    ppermute x11, starting transfers between devices, flips(): return lax.ppermute(value, axes, [(i, i ^ bits) for i in range(size)])  19.4 us
    ppermute x9, waiting for transfers between devices, turn(): return lax.ppermute(value, axis, [(i, (i + shift) % NL) for i in range(NL)])  13.1 us
    pallas_call x14, Pallas kernels, call(): pl.pallas_call(kernel, out_shape=outs, in_specs=specs, scratch_shapes=scr...  10.9 us
    ppermute x11, waiting for transfers between devices, flips(): return lax.ppermute(value, axes, [(i, i ^ bits) for i in range(size)])  10.1 us
    all_to_all x2, starting transfers between devices, exchange(): return lax.all_to_all(block, SEQ, split_axis=0, concat_axis=0, tiled=True)  9.88 us
    all_to_all x2, waiting for transfers between devices, exchange(): return lax.all_to_all(block, SEQ, split_axis=0, concat_axis=0, tiled=True)  7.4 us
    ppermute x4, starting transfers between devices, body(): lax.ppermute(pair[z], ('yh', 'zo', 'yl'), crossing(far, z))  6.95 us
  transfers between devices with their start and end apart: 26, of which 12 were waited for; matrix products, arithmetic and copies ran while one was open for 0% of the time, Pallas kernels for 9%

profile of v3, /device:TPU:2, one launch (start us, length us, event | category | flops | bytes accessed | tf_op | source)
XLA Modules:
  0.0 110.2 jit_solution(3917235726634455252)
XLA Ops:
  2.9 3.4 %collective-permute-start.8 = (bf16[128,512]{1,0:T(8,128)(2,1)S(1)}, bf16[128,512]{1,0:T(8,128)(2,1)S(1)}, u32[]{:S(2)}, u32[]{:S(2)}) collective-permute-start(bf16[128,512]{1,0:T(8,128)(2,1)S(1)} %copy-done.3), channel_id=1, source_target_pairs={{0,32},{32,0},{64,96},{96,64},{1,33},{33,1},{65,97},{97,65},{2,34}... | collective-permute-start | bytes 393224 | tf_op jit(solution)/shard_map/ppermute | solution.py:272
  7.0 2.0 %collective-permute-start.2 = (bf16[256,128]{1,0:T(8,128)(2,1)S(1)}, bf16[256,128]{1,0:T(8,128)(2,1)S(1)}, u32[]{:S(2)}, u32[]{:S(2)}) collective-permute-start(bf16[256,128]{1,0:T(8,128)(2,1)S(1)} %bitcast.5), channel_id=1, source_target_pairs={{0,16},{4,144},{16,0},{20,128},{128,20},{132,148},{144,4},{148,132... | collective-permute-start | bytes 196616 | tf_op jit(solution)/shard_map/ppermute | solution.py:304
  9.0 4.3 %collective-permute-start.3 = (bf16[256,128]{1,0:T(8,128)(2,1)S(1)}, bf16[256,128]{1,0:T(8,128)(2,1)S(1)}, u32[]{:S(2)}, u32[]{:S(2)}) collective-permute-start(bf16[256,128]{1,0:T(8,128)(2,1)S(1)} %bitcast.8), channel_id=1, source_target_pairs={{0,4},{4,132},{16,20},{20,148},{128,0},{132,128},{144,16},{148,144... | collective-permute-start | bytes 196616 | tf_op jit(solution)/shard_map/ppermute | solution.py:304
  13.3 3.8 %collective-permute-done.3.refs_2_ = bf16[256,128]{1,0:T(8,128)(2,1)S(1)} collective-permute-done((bf16[256,128]{1,0:T(8,128)(2,1)S(1)}, bf16[256,128]{1,0:T(8,128)(2,1)S(1)}, u32[]{:S(2)}, u32[]{:S(2)}) %collective-permute-start.3) | collective-permute-done | bytes 65568 | tf_op jit(solution)/shard_map/ppermute | solution.py:304
  17.1 2.8 %collective-permute-done.4.refs_3_ = bf16[256,128]{1,0:T(8,128)(2,1)S(1)} collective-permute-done((bf16[256,128]{1,0:T(8,128)(2,1)S(1)}, bf16[256,128]{1,0:T(8,128)(2,1)S(1)}, u32[]{:S(2)}, u32[]{:S(2)}) %collective-permute-start.4) | collective-permute-done | bytes 65568 | tf_op jit(solution)/shard_map/ppermute | solution.py:304
  20.6 2.4 %collective-permute-start.6 = (bf16[1024,128]{1,0:T(8,128)(2,1)S(1)}, bf16[1024,128]{1,0:T(8,128)(2,1)S(1)}, u32[]{:S(2)}, u32[]{:S(2)}) collective-permute-start(bf16[1024,128]{1,0:T(8,128)(2,1)S(1)} %shard_map.129.q0.refs_4_), channel_id=1, source_target_pairs={{0,2},{1,3},{2,0},{3,1},{4,6},{5,7},{6,4},{7,5},{8,10},{9,11},{10,... | collective-permute-start | bytes 786440 | tf_op jit(solution)/shard_map/ppermute | solution.py:276
  24.8 5.3 %collective-permute-start.9 = (bf16[256,512]{1,0:T(8,128)(2,1)S(1)}, bf16[256,512]{1,0:T(8,128)(2,1)S(1)}, u32[]{:S(2)}, u32[]{:S(2)}) collective-permute-start(bf16[256,512]{1,0:T(8,128)(2,1)S(1)} %shard_map.130), channel_id=1, source_target_pairs={{0,64},{32,96},{64,0},{96,32},{1,65},{33,97},{65,1},{97,33},{2,66}... | collective-permute-start | bytes 786440 | tf_op jit(solution)/shard_map/ppermute | solution.py:272
  31.7 3.9 %all-to-all-start = ((bf16[32,48,128]{2,1,0:T(8,128)(2,1)}), bf16[32,48,128]{2,1,0:T(8,128)(2,1)S(1)}, u32[]{:S(2)}, u32[]{:S(2)}) async-start(bf16[32,48,128]{2,1,0:T(8,128)(2,1)} %shard_map.133), calls=%async_computation | async-start | bytes 786432 | tf_op jit(solution)/shard_map/all_to_all | solution.py:284
  35.6 6.1 %collective-permute-done.9.w2 = bf16[256,512]{1,0:T(8,128)(2,1)S(1)} collective-permute-done((bf16[256,512]{1,0:T(8,128)(2,1)S(1)}, bf16[256,512]{1,0:T(8,128)(2,1)S(1)}, u32[]{:S(2)}, u32[]{:S(2)}) %collective-permute-start.9) | collective-permute-done | bytes 262176 | tf_op jit(solution)/shard_map/ppermute | solution.py:272
  45.0 4.9 %collective-permute-start.13 = (bf16[64,1024]{1,0:T(8,128)(2,1)S(1)}, bf16[64,1024]{1,0:T(8,128)(2,1)S(1)}, u32[]{:S(2)}, u32[]{:S(2)}) collective-permute-start(bf16[64,1024]{1,0:T(8,128)(2,1)S(1)} %get-tuple-element.40), channel_id=1, source_target_pairs={{0,144},{16,128},{128,16},{144,0},{1,145},{17,129},{129,17},{145,1... | collective-permute-start | bytes 393224 | tf_op jit(solution)/shard_map/ppermute | solution.py:272
  49.9 3.1 %all-to-all-done.both = bf16[32,48,128]{2,1,0:T(8,128)(2,1)S(1)} async-done(((bf16[32,48,128]{2,1,0:T(8,128)(2,1)}), bf16[32,48,128]{2,1,0:T(8,128)(2,1)S(1)}, u32[]{:S(2)}, u32[]{:S(2)}) %all-to-all-start) | async-done | bytes 393248 | tf_op jit(solution)/shard_map/all_to_all | solution.py:284
  53.0 2.0 %shard_map.134 = (bf16[32,16,128]{2,1,0:T(8,128)(2,1)S(1)}, f32[640,256]{1,0:T(8,128)S(1)}, f32[640,256]{1,0:T(8,128)S(1)}, bf16[16,1024]{1,0:T(8,128)(2,1)S(1)}...) custom-call(bf16[32,48,128]{2,1,0:T(8,128)(2,1)S(1)} %all-to-all-done.both, ...), custom_call_target="tpu_custom_call" | custom-call | tf_op jit(solution)/shard_map/pallas_call | solution.py:261
  55.6 3.3 %collective-permute-start.14 = (bf16[32,1024]{1,0:T(8,128)(2,1)S(1)}, bf16[32,1024]{1,0:T(8,128)(2,1)S(1)}, u32[]{:S(2)}, u32[]{:S(2)}) collective-permute-start(bf16[32,1024]{1,0:T(8,128)(2,1)S(1)} %get-tuple-element.46), channel_id=1, source_target_pairs={{0,32},{32,64},{64,96},{96,0},{1,33},{33,65},{65,97},{97,1},{2,34}... | collective-permute-start | bytes 196616 | tf_op jit(solution)/shard_map/ppermute | solution.py:276
  58.9 2.1 %collective-permute-start.15 = (bf16[32,1024]{1,0:T(8,128)(2,1)S(1)}, bf16[32,1024]{1,0:T(8,128)(2,1)S(1)}, u32[]{:S(2)}, u32[]{:S(2)}) collective-permute-start(bf16[32,1024]{1,0:T(8,128)(2,1)S(1)} %get-tuple-element.47), channel_id=1, source_target_pairs={{0,64},{32,96},{64,0},{96,32},{1,65},{33,97},{65,1},{97,33},{2,66}... | collective-permute-start | bytes 196616 | tf_op jit(solution)/shard_map/ppermute | solution.py:276
  61.1 2.9 %collective-permute-start.16 = (bf16[32,1024]{1,0:T(8,128)(2,1)S(1)}, bf16[32,1024]{1,0:T(8,128)(2,1)S(1)}, u32[]{:S(2)}, u32[]{:S(2)}) collective-permute-start(bf16[32,1024]{1,0:T(8,128)(2,1)S(1)} %get-tuple-element.48), channel_id=1, source_target_pairs={{0,96},{32,0},{64,32},{96,64},{1,97},{33,1},{65,33},{97,65},{2,98}... | collective-permute-start | bytes 196616 | tf_op jit(solution)/shard_map/ppermute | solution.py:276
  63.9 3.5 %collective-permute-done.15.g2.refs_2_ = bf16[32,1024]{1,0:T(8,128)(2,1)S(1)} collective-permute-done((bf16[32,1024]{1,0:T(8,128)(2,1)S(1)}, bf16[32,1024]{1,0:T(8,128)(2,1)S(1)}, u32[]{:S(2)}, u32[]{:S(2)}) %collective-permute-start.15) | collective-permute-done | bytes 65568 | tf_op jit(solution)/shard_map/ppermute | solution.py:276
  70.3 3.4 %collective-permute-start.19 = (bf16[64,1024]{1,0:T(8,128)(2,1)S(1)}, bf16[64,1024]{1,0:T(8,128)(2,1)S(1)}, u32[]{:S(2)}, u32[]{:S(2)}) collective-permute-start(bf16[64,1024]{1,0:T(8,128)(2,1)S(1)} %shard_map.138.refs_0_), channel_id=1, source_target_pairs={{0,144},{16,128},{128,16},{144,0},{1,145},{17,129},{129,17},{145,1... | collective-permute-start | bytes 393224 | tf_op jit(solution)/shard_map/ppermute | solution.py:272
  73.7 3.2 %shard_map.136 = bf16[32,48,128]{2,1,0:T(8,128)(2,1)} custom-call(bf16[32,1024]{1,0:T(8,128)(2,1)S(1)} %get-tuple-element.45.g0.refs_0_, bf16[32,1024]{1,0:T(8,128)(2,1)S(1)} %collective-permute-done.14.g1.refs_1_, bf16[32,1024]{1,0:T(8,128)(2,1)S(1)} %collective-permute-done.15.g2.refs_2_, bf16[32,1024]{1,0:T(8,128)(2,1)S(1)} %collective-permute-done.16.g3.refs_3_, ...), custom_call_target="tpu_custom_call" | custom-call | tf_op jit(solution)/shard_map/pallas_call | solution.py:261
  76.9 6.0 %all-to-all-start.1 = ((bf16[32,48,128]{2,1,0:T(8,128)(2,1)}), bf16[32,48,128]{2,1,0:T(8,128)(2,1)S(1)}, u32[]{:S(2)}, u32[]{:S(2)}) async-start(bf16[32,48,128]{2,1,0:T(8,128)(2,1)} %shard_map.136), calls=%async_computation.1 | async-start | bytes 786432 | tf_op jit(solution)/shard_map/all_to_all | solution.py:284
  85.9 2.8 %collective-permute-start.21 = (bf16[512,128]{1,0:T(8,128)(2,1)S(1)}, bf16[512,128]{1,0:T(8,128)(2,1)S(1)}, u32[]{:S(2)}, u32[]{:S(2)}) collective-permute-start(bf16[512,128]{1,0:T(8,128)(2,1)S(1)} %get-tuple-element.58), channel_id=1, source_target_pairs={{0,32},{32,64},{64,96},{96,0},{1,33},{33,65},{65,97},{97,1},{2,34}... | collective-permute-start | bytes 393224 | tf_op jit(solution)/shard_map/ppermute | solution.py:276
  88.7 3.6 %collective-permute-start.22 = (bf16[512,128]{1,0:T(8,128)(2,1)S(1)}, bf16[512,128]{1,0:T(8,128)(2,1)S(1)}, u32[]{:S(2)}, u32[]{:S(2)}) collective-permute-start(bf16[512,128]{1,0:T(8,128)(2,1)S(1)} %get-tuple-element.59), channel_id=1, source_target_pairs={{0,64},{32,96},{64,0},{96,32},{1,65},{33,97},{65,1},{97,33},{2,66}... | collective-permute-start | bytes 393224 | tf_op jit(solution)/shard_map/ppermute | solution.py:276
  92.3 3.6 %collective-permute-start.23 = (bf16[512,128]{1,0:T(8,128)(2,1)S(1)}, bf16[512,128]{1,0:T(8,128)(2,1)S(1)}, u32[]{:S(2)}, u32[]{:S(2)}) collective-permute-start(bf16[512,128]{1,0:T(8,128)(2,1)S(1)} %get-tuple-element.60), channel_id=1, source_target_pairs={{0,96},{32,0},{64,32},{96,64},{1,97},{33,1},{65,33},{97,65},{2,98}... | collective-permute-start | bytes 393224 | tf_op jit(solution)/shard_map/ppermute | solution.py:276
  95.8 4.3 %all-to-all-done.1.outs = bf16[32,48,128]{2,1,0:T(8,128)(2,1)S(1)} async-done(((bf16[32,48,128]{2,1,0:T(8,128)(2,1)}), bf16[32,48,128]{2,1,0:T(8,128)(2,1)S(1)}, u32[]{:S(2)}, u32[]{:S(2)}) %all-to-all-start.1) | async-done | bytes 393248 | tf_op jit(solution)/shard_map/all_to_all | solution.py:284
  101.5 7.9 %collective-permute-done.22.g2 = bf16[512,128]{1,0:T(8,128)(2,1)S(1)} collective-permute-done((bf16[512,128]{1,0:T(8,128)(2,1)S(1)}, bf16[512,128]{1,0:T(8,128)(2,1)S(1)}, u32[]{:S(2)}, u32[]{:S(2)}) %collective-permute-start.22) | collective-permute-done | bytes 131104 | tf_op jit(solution)/shard_map/ppermute | solution.py:276
  (61 shorter events, 18.8 us)
Async XLA Ops:
  2.8 3.5 %collective-permute-start = (bf16[2,128,128]{2,1,0:T(8,128)(2,1)S(1)}, bf16[2,128,128]{2,1,0:T(8,128)(2,1)S(1)}, u32[]{:S(2)}, u32[]{:S(2)}) collective-permute-start(bf16[2,128,128]{2,1,0:T(8,128)(2,1)S(1)} %get-tuple-element.34), channel_id=1, source_target_pairs={{0,8},{8,0},{1,9},{9,1},{2,10},{10,2},{3,11},{11,3},{4,12},{12,4},... | collective-permute-start | bytes 196616 | tf_op jit(solution)/shard_map/ppermute | solution.py:272
  2.9 21.9 %collective-permute-start.8 = (bf16[128,512]{1,0:T(8,128)(2,1)S(1)}, bf16[128,512]{1,0:T(8,128)(2,1)S(1)}, u32[]{:S(2)}, u32[]{:S(2)}) collective-permute-start(bf16[128,512]{1,0:T(8,128)(2,1)S(1)} %copy-done.3), channel_id=1, source_target_pairs={{0,32},{32,0},{64,96},{96,64},{1,33},{33,1},{65,97},{97,65},{2,34}... | collective-permute-start | bytes 393224 | tf_op jit(solution)/shard_map/ppermute | solution.py:272
  6.3 7.0 %collective-permute-start.1 = (bf16[256,128]{1,0:T(8,128)(2,1)S(1)}, bf16[256,128]{1,0:T(8,128)(2,1)S(1)}, u32[]{:S(2)}, u32[]{:S(2)}) collective-permute-start(bf16[256,128]{1,0:T(8,128)(2,1)S(1)} %bitcast.7), channel_id=1, source_target_pairs={{0,0},{4,128},{16,16},{20,144},{128,4},{132,132},{144,20},{148,148... | collective-permute-start | bytes 196616 | tf_op jit(solution)/shard_map/ppermute | solution.py:304
  7.0 6.3 %collective-permute-start.2 = (bf16[256,128]{1,0:T(8,128)(2,1)S(1)}, bf16[256,128]{1,0:T(8,128)(2,1)S(1)}, u32[]{:S(2)}, u32[]{:S(2)}) collective-permute-start(bf16[256,128]{1,0:T(8,128)(2,1)S(1)} %bitcast.5), channel_id=1, source_target_pairs={{0,16},{4,144},{16,0},{20,128},{128,20},{132,148},{144,4},{148,132... | collective-permute-start | bytes 196616 | tf_op jit(solution)/shard_map/ppermute | solution.py:304
  9.0 8.1 %collective-permute-start.3 = (bf16[256,128]{1,0:T(8,128)(2,1)S(1)}, bf16[256,128]{1,0:T(8,128)(2,1)S(1)}, u32[]{:S(2)}, u32[]{:S(2)}) collective-permute-start(bf16[256,128]{1,0:T(8,128)(2,1)S(1)} %bitcast.8), channel_id=1, source_target_pairs={{0,4},{4,132},{16,20},{20,148},{128,0},{132,128},{144,16},{148,144... | collective-permute-start | bytes 196616 | tf_op jit(solution)/shard_map/ppermute | solution.py:304
  13.2 6.7 %collective-permute-start.4 = (bf16[256,128]{1,0:T(8,128)(2,1)S(1)}, bf16[256,128]{1,0:T(8,128)(2,1)S(1)}, u32[]{:S(2)}, u32[]{:S(2)}) collective-permute-start(bf16[256,128]{1,0:T(8,128)(2,1)S(1)} %bitcast.6), channel_id=1, source_target_pairs={{0,20},{4,148},{16,4},{20,132},{128,16},{132,144},{144,0},{148,128... | collective-permute-start | bytes 196616 | tf_op jit(solution)/shard_map/ppermute | solution.py:304
  20.0 15.6 %collective-permute-start.5 = (bf16[1024,128]{1,0:T(8,128)(2,1)S(1)}, bf16[1024,128]{1,0:T(8,128)(2,1)S(1)}, u32[]{:S(2)}, u32[]{:S(2)}) collective-permute-start(bf16[1024,128]{1,0:T(8,128)(2,1)S(1)} %shard_map.129.q0.refs_4_), channel_id=1, source_target_pairs={{0,3},{1,0},{2,1},{3,2},{4,7},{5,4},{6,5},{7,6},{8,11},{9,8},{10,9... | collective-permute-start | bytes 786440 | tf_op jit(solution)/shard_map/ppermute | solution.py:276
  20.6 15.0 %collective-permute-start.6 = (bf16[1024,128]{1,0:T(8,128)(2,1)S(1)}, bf16[1024,128]{1,0:T(8,128)(2,1)S(1)}, u32[]{:S(2)}, u32[]{:S(2)}) collective-permute-start(bf16[1024,128]{1,0:T(8,128)(2,1)S(1)} %shard_map.129.q0.refs_4_), channel_id=1, source_target_pairs={{0,2},{1,3},{2,0},{3,1},{4,6},{5,7},{6,4},{7,5},{8,10},{9,11},{10,... | collective-permute-start | bytes 786440 | tf_op jit(solution)/shard_map/ppermute | solution.py:276
  23.0 12.6 %collective-permute-start.7 = (bf16[1024,128]{1,0:T(8,128)(2,1)S(1)}, bf16[1024,128]{1,0:T(8,128)(2,1)S(1)}, u32[]{:S(2)}, u32[]{:S(2)}) collective-permute-start(bf16[1024,128]{1,0:T(8,128)(2,1)S(1)} %shard_map.129.q0.refs_4_), channel_id=1, source_target_pairs={{0,1},{1,2},{2,3},{3,0},{4,5},{5,6},{6,7},{7,4},{8,9},{9,10},{10,1... | collective-permute-start | bytes 786440 | tf_op jit(solution)/shard_map/ppermute | solution.py:276
  24.8 16.9 %collective-permute-start.9 = (bf16[256,512]{1,0:T(8,128)(2,1)S(1)}, bf16[256,512]{1,0:T(8,128)(2,1)S(1)}, u32[]{:S(2)}, u32[]{:S(2)}) collective-permute-start(bf16[256,512]{1,0:T(8,128)(2,1)S(1)} %shard_map.130), channel_id=1, source_target_pairs={{0,64},{32,96},{64,0},{96,32},{1,65},{33,97},{65,1},{97,33},{2,66}... | collective-permute-start | bytes 786440 | tf_op jit(solution)/shard_map/ppermute | solution.py:272
  31.7 21.4 %all-to-all-start = ((bf16[32,48,128]{2,1,0:T(8,128)(2,1)}), bf16[32,48,128]{2,1,0:T(8,128)(2,1)S(1)}, u32[]{:S(2)}, u32[]{:S(2)}) async-start(bf16[32,48,128]{2,1,0:T(8,128)(2,1)} %shard_map.133), calls=%async_computation | async-start | bytes 786432 | tf_op jit(solution)/shard_map/all_to_all | solution.py:284
  44.8 10.2 %collective-permute-start.11 = (bf16[64,1024]{1,0:T(8,128)(2,1)S(1)}, bf16[64,1024]{1,0:T(8,128)(2,1)S(1)}, u32[]{:S(2)}, u32[]{:S(2)}) collective-permute-start(bf16[64,1024]{1,0:T(8,128)(2,1)S(1)} %get-tuple-element.38), channel_id=1, source_target_pairs={{0,16},{16,0},{128,144},{144,128},{1,17},{17,1},{129,145},{145,129... | collective-permute-start | bytes 393224 | tf_op jit(solution)/shard_map/ppermute | solution.py:272
  44.9 10.6 %collective-permute-start.12 = (bf16[64,1024]{1,0:T(8,128)(2,1)S(1)}, bf16[64,1024]{1,0:T(8,128)(2,1)S(1)}, u32[]{:S(2)}, u32[]{:S(2)}) collective-permute-start(bf16[64,1024]{1,0:T(8,128)(2,1)S(1)} %get-tuple-element.39), channel_id=1, source_target_pairs={{0,128},{16,144},{128,0},{144,16},{1,129},{17,145},{129,1},{145,17... | collective-permute-start | bytes 393224 | tf_op jit(solution)/shard_map/ppermute | solution.py:272
  45.0 10.5 %collective-permute-start.13 = (bf16[64,1024]{1,0:T(8,128)(2,1)S(1)}, bf16[64,1024]{1,0:T(8,128)(2,1)S(1)}, u32[]{:S(2)}, u32[]{:S(2)}) collective-permute-start(bf16[64,1024]{1,0:T(8,128)(2,1)S(1)} %get-tuple-element.40), channel_id=1, source_target_pairs={{0,144},{16,128},{128,16},{144,0},{1,145},{17,129},{129,17},{145,1... | collective-permute-start | bytes 393224 | tf_op jit(solution)/shard_map/ppermute | solution.py:272
  55.6 8.3 %collective-permute-start.14 = (bf16[32,1024]{1,0:T(8,128)(2,1)S(1)}, bf16[32,1024]{1,0:T(8,128)(2,1)S(1)}, u32[]{:S(2)}, u32[]{:S(2)}) collective-permute-start(bf16[32,1024]{1,0:T(8,128)(2,1)S(1)} %get-tuple-element.46), channel_id=1, source_target_pairs={{0,32},{32,64},{64,96},{96,0},{1,33},{33,65},{65,97},{97,1},{2,34}... | collective-permute-start | bytes 196616 | tf_op jit(solution)/shard_map/ppermute | solution.py:276
  58.9 8.5 %collective-permute-start.15 = (bf16[32,1024]{1,0:T(8,128)(2,1)S(1)}, bf16[32,1024]{1,0:T(8,128)(2,1)S(1)}, u32[]{:S(2)}, u32[]{:S(2)}) collective-permute-start(bf16[32,1024]{1,0:T(8,128)(2,1)S(1)} %get-tuple-element.47), channel_id=1, source_target_pairs={{0,64},{32,96},{64,0},{96,32},{1,65},{33,97},{65,1},{97,33},{2,66}... | collective-permute-start | bytes 196616 | tf_op jit(solution)/shard_map/ppermute | solution.py:276
  61.1 7.6 %collective-permute-start.16 = (bf16[32,1024]{1,0:T(8,128)(2,1)S(1)}, bf16[32,1024]{1,0:T(8,128)(2,1)S(1)}, u32[]{:S(2)}, u32[]{:S(2)}) collective-permute-start(bf16[32,1024]{1,0:T(8,128)(2,1)S(1)} %get-tuple-element.48), channel_id=1, source_target_pairs={{0,96},{32,0},{64,32},{96,64},{1,97},{33,1},{65,33},{97,65},{2,98}... | collective-permute-start | bytes 196616 | tf_op jit(solution)/shard_map/ppermute | solution.py:276
  68.7 14.3 %collective-permute-start.17 = (bf16[64,1024]{1,0:T(8,128)(2,1)S(1)}, bf16[64,1024]{1,0:T(8,128)(2,1)S(1)}, u32[]{:S(2)}, u32[]{:S(2)}) collective-permute-start(bf16[64,1024]{1,0:T(8,128)(2,1)S(1)} %shard_map.138.refs_0_), channel_id=1, source_target_pairs={{0,16},{16,0},{128,144},{144,128},{1,17},{17,1},{129,145},{145,129... | collective-permute-start | bytes 393224 | tf_op jit(solution)/shard_map/ppermute | solution.py:272
  69.4 13.5 %collective-permute-start.18 = (bf16[64,1024]{1,0:T(8,128)(2,1)S(1)}, bf16[64,1024]{1,0:T(8,128)(2,1)S(1)}, u32[]{:S(2)}, u32[]{:S(2)}) collective-permute-start(bf16[64,1024]{1,0:T(8,128)(2,1)S(1)} %shard_map.138.refs_0_), channel_id=1, source_target_pairs={{0,128},{16,144},{128,0},{144,16},{1,129},{17,145},{129,1},{145,17... | collective-permute-start | bytes 393224 | tf_op jit(solution)/shard_map/ppermute | solution.py:272
  70.3 12.6 %collective-permute-start.19 = (bf16[64,1024]{1,0:T(8,128)(2,1)S(1)}, bf16[64,1024]{1,0:T(8,128)(2,1)S(1)}, u32[]{:S(2)}, u32[]{:S(2)}) collective-permute-start(bf16[64,1024]{1,0:T(8,128)(2,1)S(1)} %shard_map.138.refs_0_), channel_id=1, source_target_pairs={{0,144},{16,128},{128,16},{144,0},{1,145},{17,129},{129,17},{145,1... | collective-permute-start | bytes 393224 | tf_op jit(solution)/shard_map/ppermute | solution.py:272
  76.9 23.2 %all-to-all-start.1 = ((bf16[32,48,128]{2,1,0:T(8,128)(2,1)}), bf16[32,48,128]{2,1,0:T(8,128)(2,1)S(1)}, u32[]{:S(2)}, u32[]{:S(2)}) async-start(bf16[32,48,128]{2,1,0:T(8,128)(2,1)} %shard_map.136), calls=%async_computation.1 | async-start | bytes 786432 | tf_op jit(solution)/shard_map/all_to_all | solution.py:284
  85.9 15.5 %collective-permute-start.21 = (bf16[512,128]{1,0:T(8,128)(2,1)S(1)}, bf16[512,128]{1,0:T(8,128)(2,1)S(1)}, u32[]{:S(2)}, u32[]{:S(2)}) collective-permute-start(bf16[512,128]{1,0:T(8,128)(2,1)S(1)} %get-tuple-element.58), channel_id=1, source_target_pairs={{0,32},{32,64},{64,96},{96,0},{1,33},{33,65},{65,97},{97,1},{2,34}... | collective-permute-start | bytes 393224 | tf_op jit(solution)/shard_map/ppermute | solution.py:276
  88.7 20.7 %collective-permute-start.22 = (bf16[512,128]{1,0:T(8,128)(2,1)S(1)}, bf16[512,128]{1,0:T(8,128)(2,1)S(1)}, u32[]{:S(2)}, u32[]{:S(2)}) collective-permute-start(bf16[512,128]{1,0:T(8,128)(2,1)S(1)} %get-tuple-element.59), channel_id=1, source_target_pairs={{0,64},{32,96},{64,0},{96,32},{1,65},{33,97},{65,1},{97,33},{2,66}... | collective-permute-start | bytes 393224 | tf_op jit(solution)/shard_map/ppermute | solution.py:276
  92.3 17.1 %collective-permute-start.23 = (bf16[512,128]{1,0:T(8,128)(2,1)S(1)}, bf16[512,128]{1,0:T(8,128)(2,1)S(1)}, u32[]{:S(2)}, u32[]{:S(2)}) collective-permute-start(bf16[512,128]{1,0:T(8,128)(2,1)S(1)} %get-tuple-element.60), channel_id=1, source_target_pairs={{0,96},{32,0},{64,32},{96,64},{1,97},{33,1},{65,33},{97,65},{2,98}... | collective-permute-start | bytes 393224 | tf_op jit(solution)/shard_map/ppermute | solution.py:276
  (11 other events, 65.7 us)

commit v4 on v3

--- a/solution.py
+++ b/solution.py
@@ -177,7 +177,7 @@
             m[:, j * BLK:(j + 1) * BLK] = act[rows_at(block_of((here("zl") + s) % NL, j), GRP), :]
 
 
-def grad_kernel(g0, g1, g2, g3, both, conv, taps_f, prod_f, tab, trig, out_ref, rows, work):
+def grad_kernel(_, g0, g1, g2, g3, both, conv, taps_f, prod_f, tab, trig, out_ref, rows, work):
     for s, g in enumerate((g0, g1, g2, g3)):
         for j in range(8):
             rows[rows_at(block_of((here("zl") + NL - s) % NL, j), GRP), :] = g[:GRP, j * BLK:(j + 1) * BLK].astype(F32)
@@ -223,13 +223,14 @@
         out[GRP:] = m[...]
 
 
-def mm2_kernel(cols, own, sib, o0, o1, o2, o3, mall, full):
-    for core, src in enumerate((own, sib)):
+def mm2_kernel(cols, *refs):
+    o0, o1, o2, o3, mall, full = refs[8:]
+    for core, src in enumerate((refs[:4], refs[4:8])):
         for r in range(4):
             for s in range(NL):
                 b = flip(here("yh"), r // 2) * 16 + flip(here("zo"), r % 2) * 8 + flip(here("c"), core) * 4
                 b = b + (here("zl") + NL - s) % NL
-                mall[rows_at(b, GRP), :] = src[(r * NL + s) * GRP:(r * NL + s + 1) * GRP, :]
+                mall[rows_at(b, GRP), :] = src[r][s * GRP:(s + 1) * GRP, :]
     full[...] = dot(mall[...], cols[...])
     base = here("zl") - here("x") + NL
     for s, out in enumerate((o0, o1, o2, o3)):
@@ -324,18 +325,18 @@
     grads = [grads[0]] + [turn(grads[s], "zl", s) for s in range(1, NL)]
 
     act = call(half_kernel, SDS((4 * GRP, TOK), BF), *grads)
-    group = call(join_kernel, SDS((WID // 2, TOK), BF), act, *[flips(act, ("yh", "zo"), b) for b in (1, 2, 3)])
-    sibling = flips(group, ("c",), 1)
+    group = [act] + [flips(act, ("yh", "zo"), b) for b in (1, 2, 3)]
+    sibling = [flips(v, ("c",), 1) for v in group]
     tall = SDS((WID, BLK), BF)
     sums = call(
-        mm2_kernel, (SDS((WID, BLK), F32), tall, tall, tall), cols, group, sibling,
+        mm2_kernel, (SDS((WID, BLK), F32), tall, tall, tall), cols, *group, *sibling,
         scratch=[((WID, TOK), BF), ((WID, WID), F32)],
     )
     sums = [sums[0]] + [turn(sums[s], "zl", s) for s in range(1, NL)]
     grad_weight = call(sum3_kernel, rows32, *sums)
 
     outs = call(
-        grad_kernel, SDS((NBLK, 3 * GRP, BLK), BF), *grads, both, conv, taps_f, prod_f, tab, trig, scratch=conv_scratch)
+        grad_kernel, SDS((NBLK, 3 * GRP, BLK), BF), group[1], *grads, both, conv, taps_f, prod_f, tab, trig, scratch=conv_scratch, far=1)
     outs = exchange(outs)
     grad_gate_out, grad_gate_in, grad_value, grad_filter = call(
         post_kernel, (rows, rows, rows, rows32), outs, gate_in, value_in)

time: 111 us -> 123 us (1.11)
  waiting for transfers between devices: 37.2 us -> 50.3 us
    ppermute x11 -> x14, waiting for transfers between devices: 10.1 us -> 26 us  [flips(): return lax.ppermute(value, axes, [(i, i ^ bits) for i in range(size)])]
    all_to_all x2, waiting for transfers between devices: 7.4 us -> 3.14 us  [exchange(): return lax.all_to_all(block, SEQ, split_axis=0, concat_axis=0, tiled=True)]
    ppermute x9, starting transfers between devices: 23.1 us -> 21.5 us  [turn(): return lax.ppermute(value, axis, [(i, (i + shift) % NL) for i in range(NL)])]
    ppermute x9, waiting for transfers between devices: 13.1 us -> 14.5 us  [turn(): return lax.ppermute(value, axis, [(i, (i + shift) % NL) for i in range(NL)])]
    ppermute x11 -> x14, starting transfers between devices: 19.4 us -> 19.9 us  [flips(): return lax.ppermute(value, axes, [(i, i ^ bits) for i in range(size)])]
    pallas_call x14 -> x13, Pallas kernels: 10.9 us -> 10.9 us  [call(): pl.pallas_call(kernel, out_shape=outs, in_specs=specs, scratch_shapes=scr...]
  transfers between devices with their start and end apart: 26 -> 29, of which waited for: 12 -> 14; matrix products, arithmetic and copies ran while one was open for 0% -> 0% of each run, Pallas kernels for 9% -> 5%
where the time goes in v4:
time: 123 us; the launch traced here: 122 us
  starting transfers between devices  58.4 us (47%)
  waiting for transfers between devices  50.3 us (41%)
  Pallas kernels  10.9 us (9%)
  local copies, waits for them, and re-layouts  1.92 us (2%)
    ppermute x14, waiting for transfers between devices, flips(): return lax.ppermute(value, axes, [(i, i ^ bits) for i in range(size)])  26 us
    ppermute x9, starting transfers between devices, turn(): return lax.ppermute(value, axis, [(i, (i + shift) % NL) for i in range(NL)])  21.5 us
    ppermute x14, starting transfers between devices, flips(): return lax.ppermute(value, axes, [(i, i ^ bits) for i in range(size)])  19.9 us
    ppermute x9, waiting for transfers between devices, turn(): return lax.ppermute(value, axis, [(i, (i + shift) % NL) for i in range(NL)])  14.5 us
    pallas_call x13, Pallas kernels, call(): pl.pallas_call(kernel, out_shape=outs, in_specs=specs, scratch_shapes=scr...  10.9 us
    all_to_all x2, starting transfers between devices, exchange(): return lax.all_to_all(block, SEQ, split_axis=0, concat_axis=0, tiled=True)  10 us
    ppermute x4, starting transfers between devices, body(): lax.ppermute(pair[z], ('yh', 'zo', 'yl'), crossing(far, z))  6.95 us
    ppermute x4, waiting for transfers between devices, body(): lax.ppermute(pair[z], ('yh', 'zo', 'yl'), crossing(far, z))  6.66 us
  transfers between devices with their start and end apart: 29, of which 14 were waited for; matrix products, arithmetic and copies ran while one was open for 0% of the time, Pallas kernels for 5%

profile of v4, /device:TPU:2, one launch (start us, length us, event | category | flops | bytes accessed | tf_op | source)
XLA Modules:
  0.0 122.4 jit_solution(16012437757991330513)
XLA Ops:
  2.9 3.4 %collective-permute-start.8 = (bf16[128,512]{1,0:T(8,128)(2,1)S(1)}, bf16[128,512]{1,0:T(8,128)(2,1)S(1)}, u32[]{:S(2)}, u32[]{:S(2)}) collective-permute-start(bf16[128,512]{1,0:T(8,128)(2,1)S(1)} %copy-done.3), channel_id=1, source_target_pairs={{0,32},{32,0},{64,96},{96,64},{1,33},{33,1},{65,97},{97,65},{2,34}... | collective-permute-start | bytes 393224 | tf_op jit(solution)/shard_map/ppermute | solution.py:273
  9.0 4.3 %collective-permute-start.3 = (bf16[256,128]{1,0:T(8,128)(2,1)S(1)}, bf16[256,128]{1,0:T(8,128)(2,1)S(1)}, u32[]{:S(2)}, u32[]{:S(2)}) collective-permute-start(bf16[256,128]{1,0:T(8,128)(2,1)S(1)} %bitcast.8), channel_id=1, source_target_pairs={{0,4},{4,132},{16,20},{20,148},{128,0},{132,128},{144,16},{148,144... | collective-permute-start | bytes 196616 | tf_op jit(solution)/shard_map/ppermute | solution.py:305
  13.3 3.8 %collective-permute-done.3.refs_2_ = bf16[256,128]{1,0:T(8,128)(2,1)S(1)} collective-permute-done((bf16[256,128]{1,0:T(8,128)(2,1)S(1)}, bf16[256,128]{1,0:T(8,128)(2,1)S(1)}, u32[]{:S(2)}, u32[]{:S(2)}) %collective-permute-start.3) | collective-permute-done | bytes 65568 | tf_op jit(solution)/shard_map/ppermute | solution.py:305
  17.1 2.8 %collective-permute-done.4.refs_3_ = bf16[256,128]{1,0:T(8,128)(2,1)S(1)} collective-permute-done((bf16[256,128]{1,0:T(8,128)(2,1)S(1)}, bf16[256,128]{1,0:T(8,128)(2,1)S(1)}, u32[]{:S(2)}, u32[]{:S(2)}) %collective-permute-start.4) | collective-permute-done | bytes 65568 | tf_op jit(solution)/shard_map/ppermute | solution.py:305
  20.6 2.4 %collective-permute-start.6 = (bf16[1024,128]{1,0:T(8,128)(2,1)S(1)}, bf16[1024,128]{1,0:T(8,128)(2,1)S(1)}, u32[]{:S(2)}, u32[]{:S(2)}) collective-permute-start(bf16[1024,128]{1,0:T(8,128)(2,1)S(1)} %shard_map.129.q0.refs_4_), channel_id=1, source_target_pairs={{0,2},{1,3},{2,0},{3,1},{4,6},{5,7},{6,4},{7,5},{8,10},{9,11},{10,... | collective-permute-start | bytes 786440 | tf_op jit(solution)/shard_map/ppermute | solution.py:277
  24.8 5.3 %collective-permute-start.9 = (bf16[256,512]{1,0:T(8,128)(2,1)S(1)}, bf16[256,512]{1,0:T(8,128)(2,1)S(1)}, u32[]{:S(2)}, u32[]{:S(2)}) collective-permute-start(bf16[256,512]{1,0:T(8,128)(2,1)S(1)} %shard_map.130), channel_id=1, source_target_pairs={{0,64},{32,96},{64,0},{96,32},{1,65},{33,97},{65,1},{97,33},{2,66}... | collective-permute-start | bytes 786440 | tf_op jit(solution)/shard_map/ppermute | solution.py:273
  31.7 3.9 %all-to-all-start = ((bf16[32,48,128]{2,1,0:T(8,128)(2,1)}), bf16[32,48,128]{2,1,0:T(8,128)(2,1)S(1)}, u32[]{:S(2)}, u32[]{:S(2)}) async-start(bf16[32,48,128]{2,1,0:T(8,128)(2,1)} %shard_map.133), calls=%async_computation | async-start | bytes 786432 | tf_op jit(solution)/shard_map/all_to_all | solution.py:285
  35.6 6.1 %collective-permute-done.9.w2 = bf16[256,512]{1,0:T(8,128)(2,1)S(1)} collective-permute-done((bf16[256,512]{1,0:T(8,128)(2,1)S(1)}, bf16[256,512]{1,0:T(8,128)(2,1)S(1)}, u32[]{:S(2)}, u32[]{:S(2)}) %collective-permute-start.9) | collective-permute-done | bytes 262176 | tf_op jit(solution)/shard_map/ppermute | solution.py:273
  45.0 4.9 %collective-permute-start.13 = (bf16[64,1024]{1,0:T(8,128)(2,1)S(1)}, bf16[64,1024]{1,0:T(8,128)(2,1)S(1)}, u32[]{:S(2)}, u32[]{:S(2)}) collective-permute-start(bf16[64,1024]{1,0:T(8,128)(2,1)S(1)} %get-tuple-element.40), channel_id=1, source_target_pairs={{0,144},{16,128},{128,16},{144,0},{1,145},{17,129},{129,17},{145,1... | collective-permute-start | bytes 393224 | tf_op jit(solution)/shard_map/ppermute | solution.py:273
  49.9 3.1 %all-to-all-done.both = bf16[32,48,128]{2,1,0:T(8,128)(2,1)S(1)} async-done(((bf16[32,48,128]{2,1,0:T(8,128)(2,1)}), bf16[32,48,128]{2,1,0:T(8,128)(2,1)S(1)}, u32[]{:S(2)}, u32[]{:S(2)}) %all-to-all-start) | async-done | bytes 393248 | tf_op jit(solution)/shard_map/all_to_all | solution.py:285
  55.6 3.3 %collective-permute-start.14 = (bf16[32,1024]{1,0:T(8,128)(2,1)S(1)}, bf16[32,1024]{1,0:T(8,128)(2,1)S(1)}, u32[]{:S(2)}, u32[]{:S(2)}) collective-permute-start(bf16[32,1024]{1,0:T(8,128)(2,1)S(1)} %get-tuple-element.46), channel_id=1, source_target_pairs={{0,32},{32,64},{64,96},{96,0},{1,33},{33,65},{65,97},{97,1},{2,34}... | collective-permute-start | bytes 196616 | tf_op jit(solution)/shard_map/ppermute | solution.py:277
  58.9 2.1 %collective-permute-start.15 = (bf16[32,1024]{1,0:T(8,128)(2,1)S(1)}, bf16[32,1024]{1,0:T(8,128)(2,1)S(1)}, u32[]{:S(2)}, u32[]{:S(2)}) collective-permute-start(bf16[32,1024]{1,0:T(8,128)(2,1)S(1)} %get-tuple-element.47), channel_id=1, source_target_pairs={{0,64},{32,96},{64,0},{96,32},{1,65},{33,97},{65,1},{97,33},{2,66}... | collective-permute-start | bytes 196616 | tf_op jit(solution)/shard_map/ppermute | solution.py:277
  61.1 2.9 %collective-permute-start.16 = (bf16[32,1024]{1,0:T(8,128)(2,1)S(1)}, bf16[32,1024]{1,0:T(8,128)(2,1)S(1)}, u32[]{:S(2)}, u32[]{:S(2)}) collective-permute-start(bf16[32,1024]{1,0:T(8,128)(2,1)S(1)} %get-tuple-element.48), channel_id=1, source_target_pairs={{0,96},{32,0},{64,32},{96,64},{1,97},{33,1},{65,33},{97,65},{2,98}... | collective-permute-start | bytes 196616 | tf_op jit(solution)/shard_map/ppermute | solution.py:277
  63.9 3.5 %collective-permute-done.15.refs_2_.g2 = bf16[32,1024]{1,0:T(8,128)(2,1)S(1)} collective-permute-done((bf16[32,1024]{1,0:T(8,128)(2,1)S(1)}, bf16[32,1024]{1,0:T(8,128)(2,1)S(1)}, u32[]{:S(2)}, u32[]{:S(2)}) %collective-permute-start.15) | collective-permute-done | bytes 65568 | tf_op jit(solution)/shard_map/ppermute | solution.py:277
  69.4 4.6 %collective-permute-done.17._.refs_1_ = bf16[64,1024]{1,0:T(8,128)(2,1)S(1)} collective-permute-done((bf16[64,1024]{1,0:T(8,128)(2,1)S(1)}, bf16[64,1024]{1,0:T(8,128)(2,1)S(1)}, u32[]{:S(2)}, u32[]{:S(2)}) %collective-permute-start.17) | collective-permute-done | bytes 131104 | tf_op jit(solution)/shard_map/ppermute | solution.py:273
  74.0 3.2 %shard_map.137 = bf16[32,48,128]{2,1,0:T(8,128)(2,1)} custom-call(bf16[64,1024]{1,0:T(8,128)(2,1)S(1)} %collective-permute-done.17._.refs_1_, bf16[32,1024]{1,0:T(8,128)(2,1)S(1)} %get-tuple-element.45.refs_0_.g0, bf16[32,1024]{1,0:T(8,128)(2,1)S(1)} %collective-permute-done.14.refs_1_.g1, bf16[32,1024]{1,0:T(8,128)(2,1)S(1)} %collective-permute-done.15.refs_2_.g2, ...), custom_call_target="tpu_custom_call" | custom-call | tf_op jit(solution)/shard_map/pallas_call | solution.py:262
  77.2 6.1 %all-to-all-start.1 = ((bf16[32,48,128]{2,1,0:T(8,128)(2,1)}), bf16[32,48,128]{2,1,0:T(8,128)(2,1)S(1)}, u32[]{:S(2)}, u32[]{:S(2)}) async-start(bf16[32,48,128]{2,1,0:T(8,128)(2,1)} %shard_map.137), calls=%async_computation.1 | async-start | bytes 786432 | tf_op jit(solution)/shard_map/all_to_all | solution.py:285
  83.4 3.4 %collective-permute-start.18 = (bf16[64,1024]{1,0:T(8,128)(2,1)S(1)}, bf16[64,1024]{1,0:T(8,128)(2,1)S(1)}, u32[]{:S(2)}, u32[]{:S(2)}) collective-permute-start(bf16[64,1024]{1,0:T(8,128)(2,1)S(1)} %shard_map.136.refs_0_), channel_id=1, source_target_pairs={{0,128},{16,144},{128,0},{144,16},{1,129},{17,145},{129,1},{145,17... | collective-permute-start | bytes 393224 | tf_op jit(solution)/shard_map/ppermute | solution.py:273
  88.7 3.5 %collective-permute-done.18.refs_2_ = bf16[64,1024]{1,0:T(8,128)(2,1)S(1)} collective-permute-done((bf16[64,1024]{1,0:T(8,128)(2,1)S(1)}, bf16[64,1024]{1,0:T(8,128)(2,1)S(1)}, u32[]{:S(2)}, u32[]{:S(2)}) %collective-permute-start.18) | collective-permute-done | bytes 131104 | tf_op jit(solution)/shard_map/ppermute | solution.py:273
  92.2 8.1 %collective-permute-done.19.refs_3_ = bf16[64,1024]{1,0:T(8,128)(2,1)S(1)} collective-permute-done((bf16[64,1024]{1,0:T(8,128)(2,1)S(1)}, bf16[64,1024]{1,0:T(8,128)(2,1)S(1)}, u32[]{:S(2)}, u32[]{:S(2)}) %collective-permute-start.19) | collective-permute-done | bytes 131104 | tf_op jit(solution)/shard_map/ppermute | solution.py:273
  104.6 2.9 %collective-permute-start.25 = (bf16[512,128]{1,0:T(8,128)(2,1)S(1)}, bf16[512,128]{1,0:T(8,128)(2,1)S(1)}, u32[]{:S(2)}, u32[]{:S(2)}) collective-permute-start(bf16[512,128]{1,0:T(8,128)(2,1)S(1)} %get-tuple-element.59), channel_id=1, source_target_pairs={{0,64},{32,96},{64,0},{96,32},{1,65},{33,97},{65,1},{97,33},{2,66}... | collective-permute-start | bytes 393224 | tf_op jit(solution)/shard_map/ppermute | solution.py:277
  107.5 3.4 %collective-permute-start.26 = (bf16[512,128]{1,0:T(8,128)(2,1)S(1)}, bf16[512,128]{1,0:T(8,128)(2,1)S(1)}, u32[]{:S(2)}, u32[]{:S(2)}) collective-permute-start(bf16[512,128]{1,0:T(8,128)(2,1)S(1)} %get-tuple-element.60), channel_id=1, source_target_pairs={{0,96},{32,0},{64,32},{96,64},{1,97},{33,1},{65,33},{97,65},{2,98}... | collective-permute-start | bytes 393224 | tf_op jit(solution)/shard_map/ppermute | solution.py:277
  110.9 4.4 %collective-permute-done.25.g2 = bf16[512,128]{1,0:T(8,128)(2,1)S(1)} collective-permute-done((bf16[512,128]{1,0:T(8,128)(2,1)S(1)}, bf16[512,128]{1,0:T(8,128)(2,1)S(1)}, u32[]{:S(2)}, u32[]{:S(2)}) %collective-permute-start.25) | collective-permute-done | bytes 131104 | tf_op jit(solution)/shard_map/ppermute | solution.py:277
  115.3 5.2 %collective-permute-done.26.g3 = bf16[512,128]{1,0:T(8,128)(2,1)S(1)} collective-permute-done((bf16[512,128]{1,0:T(8,128)(2,1)S(1)}, bf16[512,128]{1,0:T(8,128)(2,1)S(1)}, u32[]{:S(2)}, u32[]{:S(2)}) %collective-permute-start.26) | collective-permute-done | bytes 131104 | tf_op jit(solution)/shard_map/ppermute | solution.py:277
  (66 shorter events, 24.8 us)
Async XLA Ops:
  2.9 21.9 %collective-permute-start.8 = (bf16[128,512]{1,0:T(8,128)(2,1)S(1)}, bf16[128,512]{1,0:T(8,128)(2,1)S(1)}, u32[]{:S(2)}, u32[]{:S(2)}) collective-permute-start(bf16[128,512]{1,0:T(8,128)(2,1)S(1)} %copy-done.3), channel_id=1, source_target_pairs={{0,32},{32,0},{64,96},{96,64},{1,33},{33,1},{65,97},{97,65},{2,34}... | collective-permute-start | bytes 393224 | tf_op jit(solution)/shard_map/ppermute | solution.py:273
  6.3 7.0 %collective-permute-start.1 = (bf16[256,128]{1,0:T(8,128)(2,1)S(1)}, bf16[256,128]{1,0:T(8,128)(2,1)S(1)}, u32[]{:S(2)}, u32[]{:S(2)}) collective-permute-start(bf16[256,128]{1,0:T(8,128)(2,1)S(1)} %bitcast.7), channel_id=1, source_target_pairs={{0,0},{4,128},{16,16},{20,144},{128,4},{132,132},{144,20},{148,148... | collective-permute-start | bytes 196616 | tf_op jit(solution)/shard_map/ppermute | solution.py:305
  9.0 8.1 %collective-permute-start.3 = (bf16[256,128]{1,0:T(8,128)(2,1)S(1)}, bf16[256,128]{1,0:T(8,128)(2,1)S(1)}, u32[]{:S(2)}, u32[]{:S(2)}) collective-permute-start(bf16[256,128]{1,0:T(8,128)(2,1)S(1)} %bitcast.8), channel_id=1, source_target_pairs={{0,4},{4,132},{16,20},{20,148},{128,0},{132,128},{144,16},{148,144... | collective-permute-start | bytes 196616 | tf_op jit(solution)/shard_map/ppermute | solution.py:305
  13.2 6.7 %collective-permute-start.4 = (bf16[256,128]{1,0:T(8,128)(2,1)S(1)}, bf16[256,128]{1,0:T(8,128)(2,1)S(1)}, u32[]{:S(2)}, u32[]{:S(2)}) collective-permute-start(bf16[256,128]{1,0:T(8,128)(2,1)S(1)} %bitcast.6), channel_id=1, source_target_pairs={{0,20},{4,148},{16,4},{20,132},{128,16},{132,144},{144,0},{148,128... | collective-permute-start | bytes 196616 | tf_op jit(solution)/shard_map/ppermute | solution.py:305
  20.0 15.6 %collective-permute-start.5 = (bf16[1024,128]{1,0:T(8,128)(2,1)S(1)}, bf16[1024,128]{1,0:T(8,128)(2,1)S(1)}, u32[]{:S(2)}, u32[]{:S(2)}) collective-permute-start(bf16[1024,128]{1,0:T(8,128)(2,1)S(1)} %shard_map.129.q0.refs_4_), channel_id=1, source_target_pairs={{0,3},{1,0},{2,1},{3,2},{4,7},{5,4},{6,5},{7,6},{8,11},{9,8},{10,9... | collective-permute-start | bytes 786440 | tf_op jit(solution)/shard_map/ppermute | solution.py:277
  20.6 15.0 %collective-permute-start.6 = (bf16[1024,128]{1,0:T(8,128)(2,1)S(1)}, bf16[1024,128]{1,0:T(8,128)(2,1)S(1)}, u32[]{:S(2)}, u32[]{:S(2)}) collective-permute-start(bf16[1024,128]{1,0:T(8,128)(2,1)S(1)} %shard_map.129.q0.refs_4_), channel_id=1, source_target_pairs={{0,2},{1,3},{2,0},{3,1},{4,6},{5,7},{6,4},{7,5},{8,10},{9,11},{10,... | collective-permute-start | bytes 786440 | tf_op jit(solution)/shard_map/ppermute | solution.py:277
  23.0 12.6 %collective-permute-start.7 = (bf16[1024,128]{1,0:T(8,128)(2,1)S(1)}, bf16[1024,128]{1,0:T(8,128)(2,1)S(1)}, u32[]{:S(2)}, u32[]{:S(2)}) collective-permute-start(bf16[1024,128]{1,0:T(8,128)(2,1)S(1)} %shard_map.129.q0.refs_4_), channel_id=1, source_target_pairs={{0,1},{1,2},{2,3},{3,0},{4,5},{5,6},{6,7},{7,4},{8,9},{9,10},{10,1... | collective-permute-start | bytes 786440 | tf_op jit(solution)/shard_map/ppermute | solution.py:277
  24.8 16.9 %collective-permute-start.9 = (bf16[256,512]{1,0:T(8,128)(2,1)S(1)}, bf16[256,512]{1,0:T(8,128)(2,1)S(1)}, u32[]{:S(2)}, u32[]{:S(2)}) collective-permute-start(bf16[256,512]{1,0:T(8,128)(2,1)S(1)} %shard_map.130), channel_id=1, source_target_pairs={{0,64},{32,96},{64,0},{96,32},{1,65},{33,97},{65,1},{97,33},{2,66}... | collective-permute-start | bytes 786440 | tf_op jit(solution)/shard_map/ppermute | solution.py:273
  31.7 21.4 %all-to-all-start = ((bf16[32,48,128]{2,1,0:T(8,128)(2,1)}), bf16[32,48,128]{2,1,0:T(8,128)(2,1)S(1)}, u32[]{:S(2)}, u32[]{:S(2)}) async-start(bf16[32,48,128]{2,1,0:T(8,128)(2,1)} %shard_map.133), calls=%async_computation | async-start | bytes 786432 | tf_op jit(solution)/shard_map/all_to_all | solution.py:285
  44.8 10.2 %collective-permute-start.11 = (bf16[64,1024]{1,0:T(8,128)(2,1)S(1)}, bf16[64,1024]{1,0:T(8,128)(2,1)S(1)}, u32[]{:S(2)}, u32[]{:S(2)}) collective-permute-start(bf16[64,1024]{1,0:T(8,128)(2,1)S(1)} %get-tuple-element.38), channel_id=1, source_target_pairs={{0,16},{16,0},{128,144},{144,128},{1,17},{17,1},{129,145},{145,129... | collective-permute-start | bytes 393224 | tf_op jit(solution)/shard_map/ppermute | solution.py:273
  44.9 10.6 %collective-permute-start.12 = (bf16[64,1024]{1,0:T(8,128)(2,1)S(1)}, bf16[64,1024]{1,0:T(8,128)(2,1)S(1)}, u32[]{:S(2)}, u32[]{:S(2)}) collective-permute-start(bf16[64,1024]{1,0:T(8,128)(2,1)S(1)} %get-tuple-element.39), channel_id=1, source_target_pairs={{0,128},{16,144},{128,0},{144,16},{1,129},{17,145},{129,1},{145,17... | collective-permute-start | bytes 393224 | tf_op jit(solution)/shard_map/ppermute | solution.py:273
  45.0 10.5 %collective-permute-start.13 = (bf16[64,1024]{1,0:T(8,128)(2,1)S(1)}, bf16[64,1024]{1,0:T(8,128)(2,1)S(1)}, u32[]{:S(2)}, u32[]{:S(2)}) collective-permute-start(bf16[64,1024]{1,0:T(8,128)(2,1)S(1)} %get-tuple-element.40), channel_id=1, source_target_pairs={{0,144},{16,128},{128,16},{144,0},{1,145},{17,129},{129,17},{145,1... | collective-permute-start | bytes 393224 | tf_op jit(solution)/shard_map/ppermute | solution.py:273
  55.6 8.3 %collective-permute-start.14 = (bf16[32,1024]{1,0:T(8,128)(2,1)S(1)}, bf16[32,1024]{1,0:T(8,128)(2,1)S(1)}, u32[]{:S(2)}, u32[]{:S(2)}) collective-permute-start(bf16[32,1024]{1,0:T(8,128)(2,1)S(1)} %get-tuple-element.46), channel_id=1, source_target_pairs={{0,32},{32,64},{64,96},{96,0},{1,33},{33,65},{65,97},{97,1},{2,34}... | collective-permute-start | bytes 196616 | tf_op jit(solution)/shard_map/ppermute | solution.py:277
  58.9 8.5 %collective-permute-start.15 = (bf16[32,1024]{1,0:T(8,128)(2,1)S(1)}, bf16[32,1024]{1,0:T(8,128)(2,1)S(1)}, u32[]{:S(2)}, u32[]{:S(2)}) collective-permute-start(bf16[32,1024]{1,0:T(8,128)(2,1)S(1)} %get-tuple-element.47), channel_id=1, source_target_pairs={{0,64},{32,96},{64,0},{96,32},{1,65},{33,97},{65,1},{97,33},{2,66}... | collective-permute-start | bytes 196616 | tf_op jit(solution)/shard_map/ppermute | solution.py:277
  61.1 7.7 %collective-permute-start.16 = (bf16[32,1024]{1,0:T(8,128)(2,1)S(1)}, bf16[32,1024]{1,0:T(8,128)(2,1)S(1)}, u32[]{:S(2)}, u32[]{:S(2)}) collective-permute-start(bf16[32,1024]{1,0:T(8,128)(2,1)S(1)} %get-tuple-element.48), channel_id=1, source_target_pairs={{0,96},{32,0},{64,32},{96,64},{1,97},{33,1},{65,33},{97,65},{2,98}... | collective-permute-start | bytes 196616 | tf_op jit(solution)/shard_map/ppermute | solution.py:277
  77.2 44.2 %all-to-all-start.1 = ((bf16[32,48,128]{2,1,0:T(8,128)(2,1)}), bf16[32,48,128]{2,1,0:T(8,128)(2,1)S(1)}, u32[]{:S(2)}, u32[]{:S(2)}) async-start(bf16[32,48,128]{2,1,0:T(8,128)(2,1)} %shard_map.137), calls=%async_computation.1 | async-start | bytes 786432 | tf_op jit(solution)/shard_map/all_to_all | solution.py:285
  83.4 8.9 %collective-permute-start.18 = (bf16[64,1024]{1,0:T(8,128)(2,1)S(1)}, bf16[64,1024]{1,0:T(8,128)(2,1)S(1)}, u32[]{:S(2)}, u32[]{:S(2)}) collective-permute-start(bf16[64,1024]{1,0:T(8,128)(2,1)S(1)} %shard_map.136.refs_0_), channel_id=1, source_target_pairs={{0,128},{16,144},{128,0},{144,16},{1,129},{17,145},{129,1},{145,17... | collective-permute-start | bytes 393224 | tf_op jit(solution)/shard_map/ppermute | solution.py:273
  86.7 13.6 %collective-permute-start.19 = (bf16[64,1024]{1,0:T(8,128)(2,1)S(1)}, bf16[64,1024]{1,0:T(8,128)(2,1)S(1)}, u32[]{:S(2)}, u32[]{:S(2)}) collective-permute-start(bf16[64,1024]{1,0:T(8,128)(2,1)S(1)} %shard_map.136.refs_0_), channel_id=1, source_target_pairs={{0,144},{16,128},{128,16},{144,0},{1,145},{17,129},{129,17},{145,1... | collective-permute-start | bytes 393224 | tf_op jit(solution)/shard_map/ppermute | solution.py:273
  88.2 12.1 %collective-permute-start.20 = (bf16[64,1024]{1,0:T(8,128)(2,1)S(1)}, bf16[64,1024]{1,0:T(8,128)(2,1)S(1)}, u32[]{:S(2)}, u32[]{:S(2)}) collective-permute-start(bf16[64,1024]{1,0:T(8,128)(2,1)S(1)} %shard_map.136.refs_0_), channel_id=1, source_target_pairs={{0,8},{8,0},{1,9},{9,1},{2,10},{10,2},{3,11},{11,3},{4,12},{12,4},... | collective-permute-start | bytes 393224 | tf_op jit(solution)/shard_map/ppermute | solution.py:273
  88.2 12.1 %collective-permute-start.21 = (bf16[64,1024]{1,0:T(8,128)(2,1)S(1)}, bf16[64,1024]{1,0:T(8,128)(2,1)S(1)}, u32[]{:S(2)}, u32[]{:S(2)}) collective-permute-start(bf16[64,1024]{1,0:T(8,128)(2,1)S(1)} %collective-permute-done.17._.refs_1_), channel_id=1, source_target_pairs={{0,8},{8,0},{1,9},{9,1},{2,10},{10,2},{3,11},{11,3},{4,12},{12,4},... | collective-permute-start | bytes 393224 | tf_op jit(solution)/shard_map/ppermute | solution.py:273
  92.2 8.1 %collective-permute-start.22 = (bf16[64,1024]{1,0:T(8,128)(2,1)S(1)}, bf16[64,1024]{1,0:T(8,128)(2,1)S(1)}, u32[]{:S(2)}, u32[]{:S(2)}) collective-permute-start(bf16[64,1024]{1,0:T(8,128)(2,1)S(1)} %collective-permute-done.18.refs_2_), channel_id=1, source_target_pairs={{0,8},{8,0},{1,9},{9,1},{2,10},{10,2},{3,11},{11,3},{4,12},{12,4},... | collective-permute-start | bytes 393224 | tf_op jit(solution)/shard_map/ppermute | solution.py:273
  102.6 8.3 %collective-permute-start.24 = (bf16[512,128]{1,0:T(8,128)(2,1)S(1)}, bf16[512,128]{1,0:T(8,128)(2,1)S(1)}, u32[]{:S(2)}, u32[]{:S(2)}) collective-permute-start(bf16[512,128]{1,0:T(8,128)(2,1)S(1)} %get-tuple-element.58), channel_id=1, source_target_pairs={{0,32},{32,64},{64,96},{96,0},{1,33},{33,65},{65,97},{97,1},{2,34}... | collective-permute-start | bytes 393224 | tf_op jit(solution)/shard_map/ppermute | solution.py:277
  104.6 10.7 %collective-permute-start.25 = (bf16[512,128]{1,0:T(8,128)(2,1)S(1)}, bf16[512,128]{1,0:T(8,128)(2,1)S(1)}, u32[]{:S(2)}, u32[]{:S(2)}) collective-permute-start(bf16[512,128]{1,0:T(8,128)(2,1)S(1)} %get-tuple-element.59), channel_id=1, source_target_pairs={{0,64},{32,96},{64,0},{96,32},{1,65},{33,97},{65,1},{97,33},{2,66}... | collective-permute-start | bytes 393224 | tf_op jit(solution)/shard_map/ppermute | solution.py:277
  107.5 13.1 %collective-permute-start.26 = (bf16[512,128]{1,0:T(8,128)(2,1)S(1)}, bf16[512,128]{1,0:T(8,128)(2,1)S(1)}, u32[]{:S(2)}, u32[]{:S(2)}) collective-permute-start(bf16[512,128]{1,0:T(8,128)(2,1)S(1)} %get-tuple-element.60), channel_id=1, source_target_pairs={{0,96},{32,0},{64,32},{96,64},{1,97},{33,1},{65,33},{97,65},{2,98}... | collective-permute-start | bytes 393224 | tf_op jit(solution)/shard_map/ppermute | solution.py:277
  (14 other events, 80.1 us)
